TPU v7x, 32 devices: a whole 2x2x4 slice. The times are simulated.
32 devices in a mesh: gx: 4 (over y, x), gy: 8 (over z, core).
Axes of the slice: x: 2, y: 2, z: 4, core: 2. Of those that a mesh axis runs over, the one named last changes fastest.
Arguments:
- pressure: float32 [2, 512, 1024], P(None, 'gx', 'gy'), may hold values from 0.5 to 1.5
- saturations: float32 [2, 2, 512, 1024], P(None, None, 'gx', 'gy'), may hold values from 0.05 to 0.4
- old_mass: float32 [3, 2, 512, 1024], P(None, None, 'gx', 'gy'), may hold values from 0 to 0.4
- pore_volume: float32 [2, 512, 1024], P(None, 'gx', 'gy'), may hold values from 0.3 to 3
- transmissibility: float32 [3, 2, 512, 1024], P(None, None, 'gx', 'gy'), may hold values from 0.3 to 3
- direction: float32 [3, 2, 512, 1024], P(None, None, 'gx', 'gy'), may hold values from -6 to 6
- seg_pressure: float32 [128, 128], P('gx'), may hold values from 0.4 to 1.2
- seg_direction: float32 [128, 128], P('gx'), may hold values from -6 to 6
- perf_cell: int32 [128, 128], P('gx'), may hold values from 0 to 262143, as said below
- well_index: float32 [128, 128], P('gx'), may hold values from 0.2 to 2
- parent: int32 [128, 128], P('gx'), may hold values from 0 to 126, as said below
- seg_head: float32 [128, 128], P('gx'), may hold values from 0 to 0.3
- well_mode: int32 [128], P('gx'), may hold values from 0 to 1
- bhp_limit: float32 [128], P('gx'), may hold values from 0.3 to 0.8
- guide_rate: float32 [128], P('gx'), may hold values from 0.5 to 5
- group_of: int32 [128, 1], P('gx'), may hold values from 0 to 127
- group_target: float32 [128], replicated, may hold values from 200 to 800
Outputs:
- cell_residual: float32 [3, 2, 512, 1024], P(None, None, 'gx', 'gy')
- cell_jvp: float32 [3, 2, 512, 1024], P(None, None, 'gx', 'gy')
- seg_residual: float32 [128, 128], P(('gx', 'gy'))
- seg_jvp: float32 [128, 128], P(('gx', 'gy'))
- group_rates: float32 [3, 128], replicated
Inputs may be any that keep to these rules, and one draw needn't show every extreme that they name: perf_cell codes (layer * 128 + xl) * 1024 + row, with xl the column within the strip of 128 columns of the well's block of 32 wells. `parent`: segment 0 of every well names itself; every other segment names a segment of lower number. `group_of`: every group has at least one well.
All inputs are finite; a program needn't handle non-finite values.
Results may differ from a plain program's by a relative error of at most 0.0003.
Values sent between devices are 32-bit elements; how exact they have to be, the bound alone decides.
No kernel may reach another device: no remote copies, remote signals or barrier semaphores. Data moves between devices by JAX's collectives and lax.ppermute only.
A program may use at most 128 MiB of HBM per device.

v0:
```python
import jax
import jax.numpy as jnp
from jax import lax
from jax.sharding import PartitionSpec as P

COMPRESS = (0.05, 0.2, 1.0)
VISCOSITY = (0.5, 1.0, 0.2)
DENSITY = (1.0, 0.8, 0.2)
ROCK_COMP = 0.01
GRAVITY = 0.05
UPWIND_WIDTH = 0.02
FRICTION = 0.002
RATE_SCALE = 0.1


def padded_2(x, sides, width):
    for axis, dim in sides:
        devices, length = (lax.axis_size(axis), x.shape[dim])
        up = [(i, (i + 1) % devices) for i in range(devices - 1)]
        down = [(j, i) for i, j in up]
        last = lax.slice_in_dim(x, length - width, length, axis=dim)
        first = lax.slice_in_dim(x, 0, width, axis=dim)
        before = lax.ppermute(last, axis, up)
        after = lax.ppermute(first, axis, down)
        x = jnp.concatenate([before, x, after], axis=dim)
    return x


def phase_props(press, water, gas):
    oil = 1.0 - water - gas
    satur = (water, oil, gas)
    rock = 1.0 + ROCK_COMP * (press - 1.0)
    mobility = []
    masses = []
    for phase in range(3):
        volume = jnp.exp(COMPRESS[phase] * (press - 1.0))
        mobility.append(satur[phase] * satur[phase] * volume / VISCOSITY[phase])
        masses.append(rock * satur[phase] * volume)
    return (jnp.stack(mobility), jnp.stack(masses))


def face_flux(press_in, press_out, mobil_in, mobil_out, trans, lift):
    fluxes = []
    for phase in range(3):
        potential = press_in - press_out + DENSITY[phase] * lift
        upwind = jax.nn.sigmoid(potential / UPWIND_WIDTH)
        fluxes.append(
            trans * (upwind * mobil_in[phase] + (1.0 - upwind) * mobil_out[phase]) * potential
        )
    return jnp.stack(fluxes)


def ancestry(parent):
    count = parent.shape[1]
    segment_ids = jnp.arange(count, dtype=jnp.int32)
    reach = (segment_ids[None, :, None] == segment_ids[None, None, :]) | (
        parent[:, None, :] == segment_ids[None, :, None]
    )
    reach = reach.astype(jnp.bfloat16)
    for level in range((count - 1).bit_length()):
        product = jnp.einsum("wsu,wut->wst", reach, reach, preferred_element_type=jnp.float32)
        reach = jnp.minimum(product, 1.0).astype(jnp.bfloat16)
    return reach.astype(jnp.float32)


def segment_terms(parent, seg_head, well_mode, bhp_limit, target):
    reach = ancestry(parent)

    def equations(total_vals, seg_vals):
        flow = jnp.einsum("wst,wt->ws", reach, total_vals, precision=lax.Precision.HIGHEST)
        above = jnp.take_along_axis(seg_vals, parent, axis=1)
        inner = seg_vals - above - seg_head - FRICTION * flow
        root = jnp.where(
            well_mode == 1, RATE_SCALE * (flow[:, 0] - target), seg_vals[:, 0] - bhp_limit
        )
        return inner.at[:, 0].set(root)

    return equations


def per_device(
    pressure,
    saturations,
    old_mass,
    pore_volume,
    transmissibility,
    direction,
    seg_pressure,
    seg_direction,
    perf_cell,
    well_index,
    parent,
    seg_head,
    well_mode,
    bhp_limit,
    guide_rate,
    group_of,
    group_target,
):
    layers, cols, rows = pressure.shape
    col_count = lax.axis_size("gx")
    row_count = lax.axis_size("gy")
    col_index = lax.axis_index("gx")
    row_index = lax.axis_index("gy")
    col_glob = col_index * cols + jnp.arange(cols, dtype=jnp.int32)
    row_glob = row_index * rows + jnp.arange(rows, dtype=jnp.int32)
    trans_cols = jnp.where(
        (col_glob == cols * col_count - 1)[None, :, None], 0.0, transmissibility[0]
    )
    trans_rows = jnp.where(
        (row_glob == rows * row_count - 1)[None, None, :], 0.0, transmissibility[1]
    )
    stacked = jnp.concatenate(
        [pressure[None], saturations, direction, trans_cols[None], trans_rows[None]], axis=0
    )
    padded = padded_2(stacked, (("gx", 2), ("gy", 3)), 1)
    state_pad = padded[0:3]
    direc_pad = padded[3:6]
    tcol_pad = padded[6]
    trow_pad = padded[7]
    all_rows = rows * row_count
    layer_span = cols * all_rows
    layer = perf_cell // layer_span
    remain = perf_cell % layer_span
    local_row = remain % all_rows - row_index * rows
    owned = (local_row >= 0) & (local_row < rows)
    flat_cell = (layer * cols + remain // all_rows) * rows + jnp.clip(local_row, 0, rows - 1)
    weight = jnp.where(owned, well_index, 0.0)

    def local_terms(state, seg_vals):
        press = state[0]
        mobility, masses = phase_props(press, state[1], state[2])
        mobil_in = mobility[:, :, 1:-1, 1:-1]
        press_in = press[:, 1:-1, 1:-1]
        residual = masses[:, :, 1:-1, 1:-1] * pore_volume - old_mass
        flux_cols = face_flux(
            press[:, :-1, 1:-1],
            press[:, 1:, 1:-1],
            mobility[:, :, :-1, 1:-1],
            mobility[:, :, 1:, 1:-1],
            tcol_pad[:, :-1, 1:-1],
            0.0,
        )
        residual = residual + flux_cols[:, :, 1:] - flux_cols[:, :, :-1]
        flux_rows = face_flux(
            press[:, 1:-1, :-1],
            press[:, 1:-1, 1:],
            mobility[:, :, 1:-1, :-1],
            mobility[:, :, 1:-1, 1:],
            trow_pad[:, 1:-1, :-1],
            0.0,
        )
        residual = residual + flux_rows[:, :, :, 1:] - flux_rows[:, :, :, :-1]
        flux_layers = face_flux(
            press_in[:-1],
            press_in[1:],
            mobil_in[:, :-1],
            mobil_in[:, 1:],
            transmissibility[2][:-1],
            GRAVITY,
        )
        residual = (
            residual
            + jnp.pad(flux_layers, ((0, 0), (0, 1), (0, 0), (0, 0)))
            - jnp.pad(flux_layers, ((0, 0), (1, 0), (0, 0), (0, 0)))
        )
        mobil_flat = mobil_in.reshape(3, -1)
        rates = weight * mobil_flat[:, flat_cell] * (press_in.reshape(-1)[flat_cell] - seg_vals)
        residual = (
            residual.reshape(3, -1)
            .at[:, flat_cell.reshape(-1)]
            .add(rates.reshape(3, -1))
            .reshape(residual.shape)
        )
        return (residual, rates)

    primal, tangent = jax.jvp(local_terms, (state_pad, seg_pressure), (direc_pad, seg_direction))
    cell_residual, rates = primal
    cell_jvp, rate_tangent = tangent
    rate_total = jnp.sum(rates, axis=0)
    total_tangent = jnp.sum(rate_tangent, axis=0)
    member = (
        group_of[:, 0][:, None] == jnp.arange(group_target.shape[0], dtype=jnp.int32)[None, :]
    ).astype(jnp.float32)
    rates_part = jnp.dot(jnp.sum(rates, axis=2), member, precision=lax.Precision.HIGHEST)
    guide_part = jnp.dot(guide_rate, member, precision=lax.Precision.HIGHEST)
    guide_total = lax.psum(guide_part, "gx")
    group_rates = lax.psum(rates_part, ("gx", "gy"))
    target = (
        jnp.dot(member, group_target, precision=lax.Precision.HIGHEST)
        * guide_rate
        / jnp.dot(member, guide_total, precision=lax.Precision.HIGHEST)
    )
    well_count = seg_pressure.shape[0]
    share = well_count // row_count
    start = row_index * share

    def pick(values):
        return lax.dynamic_slice_in_dim(values, start, share, 0)

    total_sum, tangent_sum = lax.psum((rate_total, total_tangent), "gy")
    equations = segment_terms(parent, seg_head, well_mode, bhp_limit, target)
    seg_full, seg_tan = jax.jvp(equations, (total_sum, seg_pressure), (tangent_sum, seg_direction))
    seg_residual = pick(seg_full)
    seg_jvp = pick(seg_tan)
    return (cell_residual, cell_jvp, seg_residual, seg_jvp, group_rates)


def solution(mesh):
    placed = (
        P(None, "gx", "gy"),
        P(None, None, "gx", "gy"),
        P(None, None, "gx", "gy"),
        P(None, "gx", "gy"),
        P(None, None, "gx", "gy"),
        P(None, None, "gx", "gy"),
        P("gx", None),
        P("gx", None),
        P("gx", None),
        P("gx", None),
        P("gx", None),
        P("gx", None),
        P("gx"),
        P("gx"),
        P("gx"),
        P("gx", None),
        P(),
    )
    return jax.shard_map(
        per_device,
        mesh=mesh,
        in_specs=placed,
        out_specs=(
            P(None, None, "gx", "gy"),
            P(None, None, "gx", "gy"),
            P(("gx", "gy"), None),
            P(("gx", "gy"), None),
            P(),
        ),
        check_vma=False,
    )
```

profile of v0, /device:TPU:0, one launch (start us, length us, event | category | flops | bytes accessed | tf_op | source)
XLA Modules:
  0.0 424.8 jit_solution(18046167283331318950)
XLA Ops:
  0.7 0.9 bitcast_dynamic-update-slice_fusion
  1.7 1.0 constant_dynamic-update-slice_fusion.1
  2.6 1.0 constant_dynamic-update-slice_fusion
  3.7 1.0 select_dynamic-update-slice_fusion.1
  4.7 0.9 select_dynamic-update-slice_fusion
  5.6 1.3 collective-permute-start.1
  6.9 5.5 %collective-permute-start = (f32[8,2,1,128]{3,2,1,0:T(1,128)S(1)}, f32[8,2,1,128]{3,2,1,0:T(1,128)S(1)}, u32[]{:S(2)}, u32[]{:S(2)}) collective-permute-start(f32[8,2,1,128]{3,2,1,0:T(1,128)S(1)} %get-tuple-element.88), channel_id=1, source_target_pairs={{0,8},{8,16},{16,24},{1,9},{9,17},{17,25},{2,10},{10,18},{18,26},{... | collective-permute-start | bytes 24584 | tf_op jit(solution)/shard_map/ppermute | solution.py:23
  12.5 0.6 compare_select_fusion
  13.1 0.8 minimum_convert_fusion.6
  13.9 1.0 minimum_convert_fusion.4
  14.9 1.0 minimum_convert_fusion.2
  15.9 2.0 minimum_convert_fusion
  18.1 10.4 %psum.29 = f32[128]{0:T(128)S(1)} all-reduce(f32[128]{0:T(128)S(1)} %convolution_bitcast_fusion.1), channel_id=1, replica_groups=mesh['gx'=4,'gy'=8] {'gx'}, use_global_device_ids=true, to_apply=%region_5.6 | all-reduce | flops 128 | bytes 1024 | tf_op jit(solution)/shard_map/psum | solution.py:187
  28.4 0.7 convolution_bitcast_fusion
  29.1 0.6 slice_reduce_fusion.2
  30.2 0.6 copy.106
  30.9 1.3 collective-permute-start.3
  32.2 0.6 copy.105
  32.8 3.2 collective-permute-start.2
  36.1 43.2 %gather_fusion.5 = f32[4096]{0:T(1024)} fusion(f32[32,128]{1,0:T(8,128)S(1)} %copy-done.1, s32[4096]{0:T(1024)S(1)} %fusion.156), kind=kCustom, calls=%fused_computation.5 | custom fusion | bytes 65536 | tf_op jit(solution)/shard_map/jvp(jit(take_along_axis))/gather | solution.py:71
  79.3 25.6 %gather_fusion.4 = f32[4096]{0:T(1024)S(1)} fusion(f32[32,128]{1,0:T(8,128)S(1)} %copy-done.2, s32[4096]{0:T(1024)S(1)} %fusion.156), kind=kCustom, calls=%fused_computation.4 | custom fusion | bytes 65536 | tf_op jit(solution)/shard_map/jvp(jit(take_along_axis))/gather | solution.py:71
  105.0 0.6 compare_reduce_fusion
  106.5 1.0 pad_maximum_fusion
  108.0 1.2 fusion.39
  110.7 0.7 fusion.60
  113.0 1.0 pad_maximum_fusion.2
  114.0 0.7 pad_maximum_fusion.14
  115.1 8.6 %copy.109 = f32[3,2,128,128]{0,3,2,1:T(8,128)} copy(f32[3,2,128,128]{3,2,1,0:T(8,128)S(1)} %fusion.34) | data formatting | bytes 786432 | tf_op jit(solution)/shard_map/jvp()/sub | solution.py:163
  123.6 8.5 %copy.110 = f32[3,2,128,128]{0,3,2,1:T(8,128)} copy(f32[3,2,128,128]{3,2,1,0:T(8,128)S(1)} %get-tuple-element.106) | data formatting | bytes 786432 | tf_op jit(solution)/shard_map/jvp()/slice | solution.py:133
  132.2 16.5 %gather_fusion = f32[4096,3]{1,0:T(8,128)S(1)} fusion(f32[3,32768]{0,1:T(8,128)} %bitcast.414, s32[4096]{0:T(1024)S(1)} %get-tuple-element.69), kind=kCustom, calls=%fused_computation | custom fusion | bytes 114688 | tf_op jit(solution)/shard_map/jvp()/gather | solution.py:168
  148.7 40.6 %gather_fusion.3 = f32[4096]{0:T(1024)} fusion(f32[32768]{0:T(1024)S(1)} %bitcast.407, s32[4096]{0:T(1024)S(1)} %get-tuple-element.69), kind=kCustom, calls=%fused_computation.3 | custom fusion | bytes 49152 | tf_op jit(solution)/shard_map/jvp()/gather | solution.py:168
  189.3 23.0 %gather_fusion.1 = f32[4096]{0:T(1024)S(1)} fusion(f32[32768]{0:T(1024)S(1)} %bitcast.408, s32[4096]{0:T(1024)S(1)} %get-tuple-element.69), kind=kCustom, calls=%fused_computation.1 | custom fusion | bytes 49152 | tf_op jit(solution)/shard_map/jvp()/gather | solution.py:168
  212.3 36.5 %scatter_custom_fusion = f32[3,32768]{0,1:T(8,128)} fusion(f32[3,32768]{0,1:T(8,128)} %bitcast.409, s32[4096]{0:T(1024)} %bitcast.429, f32[4096,3]{1,0:T(8,128)S(1)} %gather_fusion, f32[4096]{0:T(1024)S(1)} %bitcast.419, f32[4096]{0:T(1024)S(1)} %bitcast.417), kind=kCustom, calls=%fused_computation.15 | custom fusion | flops 36864 | bytes 475136 | tf_op jit(solution)/shard_map/jvp()/scatter-add | solution.py:172
  248.8 10.7 %copy.115 = f32[3,2,128,128]{3,2,1,0:T(8,128)} copy(f32[3,2,128,128]{0,3,2,1:T(8,128)} %bitcast.410) | data formatting | bytes 786432
  259.5 2.5 fusion.31
  262.0 9.5 %copy.111 = f32[3,2,128,128]{0,3,2,1:T(8,128)} copy(f32[3,2,128,128]{3,2,1,0:T(8,128)} %fusion.31) | data formatting | bytes 786432 | tf_op jit(solution)/shard_map/jvp()/sub | solution.py:163
  271.5 8.5 %copy.112 = f32[3,2,128,128]{0,3,2,1:T(8,128)} copy(f32[3,2,128,128]{3,2,1,0:T(8,128)S(1)} %get-tuple-element.105) | data formatting | bytes 786432 | tf_op jit(solution)/shard_map/jvp()/slice | solution.py:133
  280.1 19.9 %gather_fusion.2 = f32[4096,3]{1,0:T(8,128)} fusion(f32[3,32768]{0,1:T(8,128)} %bitcast.415, s32[4096]{0:T(1024)S(1)} %get-tuple-element.69), kind=kCustom, calls=%fused_computation.2 | custom fusion | bytes 114688 | tf_op jit(solution)/shard_map/jvp()/gather | solution.py:168
  300.0 37.0 %scatter_custom_fusion.1 = f32[3,32768]{0,1:T(8,128)} fusion(f32[3,32768]{0,1:T(8,128)} %bitcast.411, s32[4096]{0:T(1024)} %bitcast.430, f32[4096,3]{1,0:T(8,128)} %gather_fusion.2, f32[4096,3]{1,0:T(8,128)S(1)} %gather_fusion, f32[4096]{0:T(1024)S(1)} %bitcast.425, f32[4096]{0:T(1024)S(1)} %bitcast.420, f32[4096]{0:T(1024)S(1)} %bitcast.418), kind=kCustom, calls=%fused_computation.13 | custom fusion | flops 73728 | bytes 2588672 | tf_op jit(solution)/shard_map/jvp()/scatter-add | solution.py:172
  337.0 10.6 %copy.116 = f32[3,2,128,128]{3,2,1,0:T(8,128)} copy(f32[3,2,128,128]{0,3,2,1:T(8,128)} %bitcast.412) | data formatting | bytes 786432
  347.6 4.6 %add_reduce_fusion = (f32[32,128]{1,0:T(8,128)S(1)}, f32[32,128]{1,0:T(8,128)S(1)}, f32[3,32]{0,1:T(8,128)S(1)}) fusion(f32[3,32,128]{0,2,1:T(8,128)} %bitcast.416, f32[3,32,128]{0,2,1:T(8,128)S(1)} %bitcast.413, f32[32,128]{1,0:T(8,128)S(1)} %get-tuple-element.113, f32[32,128]{1,0:T(8,128)S(1)} %get-tuple-element.114, f32[32,128]{1,0:T(8,128)S(1)} %and_select_fusion, ...), kind=kLoop, calls=%fused_computation.17 | loop fusion | flops 126880 | bytes 229760 | tf_op jit(solution)/shard_map/reduce_sum | solution.py:181
  352.3 28.5 %all-reduce.4 = (f32[32,128]{1,0:T(8,128)S(1)}, f32[32,128]{1,0:T(8,128)S(1)}) all-reduce(f32[32,128]{1,0:T(8,128)S(1)} %get-tuple-element.55, f32[32,128]{1,0:T(8,128)S(1)} %get-tuple-element.54), channel_id=1, replica_groups=mesh['gx'=4,'gy'=8] {'gy'}, use_global_device_ids=true, to_apply=%region_3.4 | all-reduce | flops 8192 | bytes 65536 | tf_op jit(solution)/shard_map/psum | solution.py:201
  380.8 1.7 fusion.175
  382.7 1.7 fusion.174
  384.9 0.7 slice_select_fusion.1
  385.8 0.6 slice_select_fusion
  386.6 0.6 constant_dynamic-slice_fusion.1
  387.9 36.8 %psum.31 = f32[3,128]{1,0:T(4,128)} all-reduce(f32[3,128]{1,0:T(4,128)S(1)} %fusion.157), channel_id=1, replica_groups=mesh['gx'=4,'gy'=8] {'gx','gy'}, use_global_device_ids=true, to_apply=%region_9.10 | all-reduce | flops 384 | bytes 3072 | tf_op jit(solution)/shard_map/psum | solution.py:188
  (89 shorter events, 7.4 us)
Async XLA Ops:
  0.6 383.9 %copy-start = (f32[128]{0:T(128)S(1)}, f32[128]{0:T(128)}, u32[]{:S(2)}) copy-start(f32[128]{0:T(128)} %param.37) | copy-start | bytes 1540
  0.6 11.8 %copy-start.8 = (s32[32,128]{1,0:T(8,128)S(1)}, s32[32,128]{1,0:T(8,128)}, u32[]{:S(2)}) copy-start(s32[32,128]{1,0:T(8,128)} %param.29) | copy-start | bytes 49156
  0.7 12.4 %copy-start.12 = (f32[32,128]{1,0:T(8,128)S(1)}, f32[32,128]{1,0:T(8,128)}, u32[]{:S(2)}) copy-start(f32[32,128]{1,0:T(8,128)} %param.30) | copy-start | bytes 49156
  0.7 12.4 %copy-start.9 = (s32[32,128]{1,0:T(8,128)S(1)}, s32[32,128]{1,0:T(8,128)}, u32[]{:S(2)}) copy-start(s32[32,128]{1,0:T(8,128)} %param.31) | copy-start | bytes 49156
  5.6 24.2 %collective-permute-start.1 = (f32[8,2,1,128]{3,2,1,0:T(1,128)S(1)}, f32[8,2,1,128]{3,2,1,0:T(1,128)S(1)}, u32[]{:S(2)}, u32[]{:S(2)}) collective-permute-start(f32[8,2,1,128]{3,2,1,0:T(1,128)S(1)} %get-tuple-element.89), channel_id=1, source_target_pairs={{8,0},{16,8},{24,16},{9,1},{17,9},{25,17},{10,2},{18,10},{26,18},{... | collective-permute-start | bytes 24584 | tf_op jit(solution)/shard_map/ppermute | solution.py:24
  6.9 22.9 %collective-permute-start = (f32[8,2,1,128]{3,2,1,0:T(1,128)S(1)}, f32[8,2,1,128]{3,2,1,0:T(1,128)S(1)}, u32[]{:S(2)}, u32[]{:S(2)}) collective-permute-start(f32[8,2,1,128]{3,2,1,0:T(1,128)S(1)} %get-tuple-element.88), channel_id=1, source_target_pairs={{0,8},{8,16},{16,24},{1,9},{9,17},{17,25},{2,10},{10,18},{18,26},{... | collective-permute-start | bytes 24584 | tf_op jit(solution)/shard_map/ppermute | solution.py:23
  15.9 2.0 copy-start.16
  15.9 2.0 copy-start.19
  15.9 13.2 %copy-start.2 = (f32[32,128]{1,0:T(8,128)S(1)}, f32[32,128]{1,0:T(8,128)}, u32[]{:S(2)}) copy-start(f32[32,128]{1,0:T(8,128)} %param.27) | copy-start | bytes 49156
  30.2 5.7 %copy-start.1 = (f32[32,128]{1,0:T(8,128)S(1)}, f32[32,128]{1,0:T(8,128)}, u32[]{:S(2)}) copy-start(f32[32,128]{1,0:T(8,128)} %param.28) | copy-start | bytes 49156
  30.9 74.7 %collective-permute-start.3 = (f32[8,2,130,1]{2,0,3,1:T(8,128)S(1)}, f32[8,2,130,1]{2,0,3,1:T(8,128)S(1)}, u32[]{:S(2)}, u32[]{:S(2)}) collective-permute-start(f32[8,2,130,1]{2,0,3,1:T(8,128)S(1)} %copy.106), channel_id=1, source_target_pairs={{1,0},{2,1},{3,2},{4,3},{5,4},{6,5},{7,6},{9,8},{10,9},{11,10},{12... | collective-permute-start | bytes 24968 | tf_op jit(solution)/shard_map/ppermute | solution.py:24
  32.8 73.3 %collective-permute-start.2 = (f32[8,2,130,1]{2,0,3,1:T(8,128)S(1)}, f32[8,2,130,1]{2,0,3,1:T(8,128)S(1)}, u32[]{:S(2)}, u32[]{:S(2)}) collective-permute-start(f32[8,2,130,1]{2,0,3,1:T(8,128)S(1)} %copy.105), channel_id=1, source_target_pairs={{0,1},{1,2},{2,3},{3,4},{4,5},{5,6},{6,7},{8,9},{9,10},{10,11},{11... | collective-permute-start | bytes 24968 | tf_op jit(solution)/shard_map/ppermute | solution.py:23
  110.7 1.2 copy-start.5
  112.9 1.8 copy-start.6
  113.0 1.8 copy-start.7
  189.3 23.0 %copy-start.11 = (f32[4096]{0:T(1024)S(1)}, f32[4096]{0:T(1024)}, u32[]{:S(2)}) copy-start(f32[4096]{0:T(1024)} %gather_fusion.3) | copy-start | bytes 49156
  248.8 10.7 %copy-start.4 = (f32[3,1,128,128]{3,2,1,0:T(8,128)S(1)}, f32[3,1,128,128]{3,2,1,0:T(8,128)}, u32[]{:S(2)}) copy-start(f32[3,1,128,128]{3,2,1,0:T(8,128)} %get-tuple-element.112) | copy-start | bytes 589828
  347.6 33.2 %copy-start.3 = (bf16[32,128,128]{2,1,0:T(8,128)(2,1)S(1)}, bf16[32,128,128]{2,1,0:T(8,128)(2,1)}, u32[]{:S(2)}) copy-start(bf16[32,128,128]{2,1,0:T(8,128)(2,1)} %minimum_convert_fusion) | copy-start | bytes 3145732
  347.6 35.0 %copy-start.10 = (f32[4096]{0:T(1024)S(1)}, f32[4096]{0:T(1024)}, u32[]{:S(2)}) copy-start(f32[4096]{0:T(1024)} %gather_fusion.5) | copy-start | bytes 49156
  352.2 32.3 %copy-start.14 = (f32[32]{0:T(128)S(1)}, f32[32]{0:T(128)}, u32[]{:S(2)}) copy-start(f32[32]{0:T(128)} %slice_reduce_fusion.2) | copy-start | bytes 388
  352.2 32.3 %copy-start.15 = (s32[32]{0:T(128)S(1)}, s32[32]{0:T(128)}, u32[]{:S(2)}) copy-start(s32[32]{0:T(128)} %param.33) | copy-start | bytes 388
  352.2 32.3 %copy-start.17 = (f32[32]{0:T(128)S(1)}, f32[32]{0:T(128)}, u32[]{:S(2)}) copy-start(f32[32]{0:T(128)} %param.35) | copy-start | bytes 388
  352.3 32.3 %copy-start.18 = (f32[32]{0:T(128)S(1)}, f32[32]{0:T(128)}, u32[]{:S(2)}) copy-start(f32[32]{0:T(128)} %param.34) | copy-start | bytes 388
  352.3 32.3 %copy-start.20 = (s32[32,1]{0,1:T(1,128)S(1)}, s32[32,1]{0,1:T(1,128)}, u32[]{:S(2)}) copy-start(s32[32,1]{0,1:T(1,128)} %param.36) | copy-start | bytes 388
  352.3 32.3 %copy-start.21 = (f32[32]{0:T(128)S(1)}, f32[32]{0:T(128)}, u32[]{:S(2)}) copy-start(f32[32]{0:T(128)} %convolution_bitcast_fusion) | copy-start | bytes 388
  352.3 32.6 %copy-start.13 = (f32[32,128]{1,0:T(8,128)S(1)}, f32[32,128]{1,0:T(8,128)}, u32[]{:S(2)}) copy-start(f32[32,128]{1,0:T(8,128)} %param.32) | copy-start | bytes 49156
where the time goes:
time: 427 us; the launch traced here: 425 us
  local copies, waits for them, and re-layouts  233 us (55%)
  other arithmetic  93.7 us (22%)
  blocking collectives  75.7 us (18%)
  starting transfers between devices  11.3 us (3%)
  matrix products  9.39 us (2%)
    scatter-add x2, other arithmetic, local_terms(): residual = residual.reshape(3, -1).at[:, flat_cell.reshape(-1)].add(rates...  73.5 us
    gather x2, local copies, waits for them, and re-layouts, equations(): above = jnp.take_along_axis(seg_vals, parent, axis=1)  68.8 us
    gather x2, local copies, waits for them, and re-layouts, local_terms(): press_in.reshape(-1)[flat_cell] - seg_vals  63.6 us
    psum x1, blocking collectives, per_device(): group_rates = lax.psum(rates_part, ('gx', 'gy'))  36.8 us
    gather x2, local copies, waits for them, and re-layouts, local_terms(): mobil_flat[:, flat_cell]  36.5 us
    psum x1, blocking collectives, per_device(): total_sum, tangent_sum = lax.psum((rate_total, total_tangent), 'gy')  28.5 us
    unnamed x49, local copies, waits for them, and re-layouts  24.4 us
    sub x2, local copies, waits for them, and re-layouts, local_terms(): residual + jnp.pad(flux_layers, ((0, 0), (0, 1), (0, 0), (0, 0)))  18.1 us
  transfers between devices with their start and end apart: 4, of which 0 were waited for; matrix products, arithmetic and copies ran while one was open for 18% of the time, Pallas kernels for 0%

commit v1 on v0

v1 whole, which is shorter than its diff:
```python
import functools

import jax
import jax.numpy as jnp
from jax import lax
from jax.experimental import pallas as pl
from jax.experimental.pallas import tpu as pltpu
from jax.sharding import PartitionSpec as P

COMPRESS = (0.05, 0.2, 1.0)
VISCOSITY = (0.5, 1.0, 0.2)
DENSITY = (1.0, 0.8, 0.2)
ROCK_COMP = 0.01
GRAVITY = 0.05
UPWIND_WIDTH = 0.02
FRICTION = 0.002
RATE_SCALE = 0.1

F32 = jnp.float32
BF16 = jnp.bfloat16
NN = (((1,), (0,)), ((), ()))
NT = (((1,), (1,)), ((), ()))


def dot(a, b, dims=NN):
    return lax.dot_general(a, b, dims, preferred_element_type=F32)


def iota(shape, dim):
    return lax.broadcasted_iota(jnp.int32, shape, dim)


def split(x, parts):
    terms = []
    for _ in range(parts):
        head = x.astype(BF16).astype(F32)
        terms.append(head)
        x = x - head
    return terms


def mobility_of(press, dpress, water, dwater, gas, dgas):
    satur = (water, 1.0 - water - gas, gas)
    dsatur = (dwater, -dwater - dgas, dgas)
    out = []
    for a in range(3):
        volume = jnp.exp(COMPRESS[a] * (press - 1.0))
        mass = satur[a] * volume
        cdp = COMPRESS[a] * dpress
        scaled = mass * (1.0 / VISCOSITY[a])
        mob = scaled * satur[a]
        dmob = scaled * (2.0 * dsatur[a] + satur[a] * cdp)
        dmass = volume * dsatur[a] + mass * cdp
        out.append((mob, dmob, mass, dmass))
    return out


def upwind_of(pot):
    return 0.5 * jnp.tanh(pot * (0.5 / UPWIND_WIDTH)) + 0.5


def face_terms(trans, pot, dpot):
    up = upwind_of(pot)
    dup = up * (1.0 - up) * (dpot * (1.0 / UPWIND_WIDTH))
    return up, dup, trans * pot, trans * dpot


def face_flux(terms, mob_in, dmob_in, mob_out, dmob_out):
    up, dup, tpot, tdpot = terms
    diff = mob_in - mob_out
    mob = mob_out + up * diff
    dmob = dmob_out + up * (dmob_in - dmob_out) + dup * diff
    return mob * tpot, dmob * tpot + mob * tdpot


def column_to_row(eye, column):
    return jnp.sum(jnp.where(eye, column, 0.0), axis=0, keepdims=True)


def located(code, all_rows, first_row):
    if all_rows & (all_rows - 1) == 0:
        lx = code >> (all_rows.bit_length() - 1)
        row = code & (all_rows - 1)
    else:
        lx = code // all_rows
        row = code - lx * all_rows
    return lx, row - first_row


def as_column(line):
    n = line.shape[1]
    diag = iota((n, n), 0) == iota((n, n), 1)
    return jnp.sum(jnp.where(diag, line, 0.0), axis=1, keepdims=True)


def list_wells(owned, active):
    wells = owned.shape[0]
    has = jnp.max(jnp.where(owned, 1.0, 0.0), axis=1, keepdims=True)
    count = jnp.int32(0)
    for part in range(0, wells, 16):
        size = min(16, wells - part)
        bit = (1 << iota((size, 1), 0)).astype(F32)
        bits = jnp.sum(has[part : part + size] * bit).astype(jnp.int32)
        for w in range(size):
            active[1 + count] = part + w
            count = count + ((bits >> w) & 1)
    active[0] = count
    for k in range(3):
        active[1 + count + k] = wells
    return count


def outer_flux(first, last, prev, after, has_prev, has_next, layers):
    def pick(x, q):
        return x[layers * q : layers * (q + 1)]

    ins = [jnp.concatenate([pick(prev, q), pick(last, q)], axis=0) for q in range(7)]
    outs = [jnp.concatenate([pick(first, q), pick(after, q)], axis=0) for q in range(6)]
    props = [mobility_of(*(x[q] for q in (0, 3, 1, 4, 2, 5))) for x in (ins, outs)]
    terms = face_terms(ins[6], ins[0] - outs[0], ins[3] - outs[3])
    fluxes = [
        face_flux(terms, props[0][a][0], props[0][a][1], props[1][a][0], props[1][a][1])
        for a in range(3)
    ]
    before = iota((2 * layers, first.shape[1]), 0) < layers
    valid = jnp.where(before, has_prev.astype(jnp.int32), has_next.astype(jnp.int32)) == 1
    return [jnp.where(valid, f, 0.0) for t in (0, 1) for f in (x[t] for x in fluxes)]


def wells_kernel(
    all_rows,
    perf_hbm,
    press_hbm,
    satur_hbm,
    direc_hbm,
    seg_p_hbm,
    seg_d_hbm,
    wi_hbm,
    guide_hbm,
    group_hbm,
    mode_hbm,
    bhp_hbm,
    group_target_hbm,
    trans_hbm,
    send,
    rates,
    rowloc,
    lxs,
    perf,
    press,
    satur,
    direc,
    seg_p,
    seg_d,
    wi,
    guide,
    group,
    mode,
    bhp,
    group_target,
    t_col,
    held,
    held_low,
    gath,
    active,
    sems,
):
    layers, cols, rows = press.shape
    cells = layers * cols
    wells, segs = seg_p.shape
    gx, gy = lax.axis_size("gx"), lax.axis_size("gy")
    xi, yi = lax.axis_index("gx"), lax.axis_index("gy")
    share = wells // gy
    moves = [
        pltpu.make_async_copy(src, dst, sems.at[k])
        for k, (src, dst) in enumerate(
            [
                (perf_hbm, perf),
                (press_hbm, press),
                (satur_hbm, satur),
                (direc_hbm, direc),
                (seg_p_hbm, seg_p),
                (seg_d_hbm, seg_d),
                (wi_hbm, wi),
                (guide_hbm, guide),
                (group_hbm, group),
                (mode_hbm, mode),
                (bhp_hbm, bhp),
                (group_target_hbm, group_target),
                (trans_hbm.at[0, :, pl.ds(cols - 8, 8), :], t_col),
            ]
        )
    ]
    for move in moves:
        move.start()

    moves[0].wait()
    lx_all, row_all = located(perf[...], all_rows, yi * rows)
    owned = (row_all >= 0) & (row_all < rows)
    nowhere = jnp.full((8, segs), -1, jnp.int32)
    lxs[0:wells, :] = lx_all
    rowloc[0:wells, :] = jnp.where(owned, row_all, -1)
    lxs[wells : wells + 8, :] = nowhere
    rowloc[wells : wells + 8, :] = nowhere
    count = list_wells(owned, active)

    for move in moves[4:]:
        move.wait()
    spot = iota((wells, 128), 1) - iota((wells, 128), 0)
    guides = jnp.where(spot == 3 * wells, as_column(guide[...]), 0.0)
    groups = jnp.where(spot == 0, as_column(group[...].astype(F32)), 0.0)
    groups = jnp.sum(groups, axis=0, keepdims=True)

    pick = iota((share, wells), 1) == iota((share, wells), 0) + yi * share

    def own(line):
        return jnp.sum(jnp.where(pick, line, 0.0), axis=1, keepdims=True)

    number = own(group[...].astype(F32))
    member = number == iota((share, 128), 1).astype(F32)
    columns = [
        own(mode[...].astype(F32)),
        own(guide[...]),
        number,
        jnp.sum(jnp.where(member, group_target[...], 0.0), axis=1, keepdims=True),
        own(bhp[...]),
    ]
    lane = iota((share, 128), 1)
    info = jnp.zeros((share, 128), F32)
    for k, column in enumerate(columns):
        info = jnp.where(lane == k, column, info)
    for q in range(6):
        rates[q, wells : wells + 8, :] = jnp.zeros((8, segs), F32)
    rates[0, wells + 4 : wells + 4 + share, :] = info

    edges = [[], []]
    fields = [press, satur.at[0], satur.at[1], direc.at[0], direc.at[1], direc.at[2]]
    arrive = {0: 1, 1: 2, 3: 3}
    for q, field in enumerate(fields):
        if q in arrive:
            moves[arrive[q]].wait()
        block = field[...].reshape(cells, rows)
        terms = split(block, 3 if q == 0 else 2)
        held[q, :, 0:rows] = terms[0].astype(BF16)
        held[q, :, rows : 2 * rows] = terms[1].astype(BF16)
        if q == 0:
            held_low[...] = terms[2].astype(BF16)
        for z in range(layers):
            edges[0].append(field[z, 0:1, :])
            edges[1].append(field[z, cols - 1 : cols, :])
    for z in range(layers):
        last = t_col[z, 7:8, :]
        edges[0].append(jnp.zeros_like(last))
        edges[1].append(last)
    chunk = send.shape[1]
    for side, step in ((0, -1), (1, 1)):
        there = xi + step
        edge = jnp.concatenate(edges[side], axis=0)

        @pl.when((there >= 0) & (there < gx))
        def _(edge=edge, to=there * gy + yi):
            send[pl.ds(to, 1), 0 : 7 * layers, :] = edge[None]

    def gather_wells(at, width):
        ids = [active[1 + at + k] for k in range(width)]
        row = jnp.concatenate([rowloc[pl.ds(w, 1), :] for w in ids], axis=1)
        lx = jnp.concatenate([lxs[pl.ds(w, 1), :] for w in ids], axis=1)
        hot = jnp.where(iota((rows, width * segs), 0) == row, 1.0, 0.0).astype(BF16)
        hot2 = jnp.concatenate([hot, hot], axis=0)
        here = iota((cells, width * segs), 0) == lx
        for q in range(len(fields)):
            found = dot(held[q], hot2)
            if q == 0:
                found = found + dot(held_low[...], hot)
            line = jnp.sum(jnp.where(here, found, 0.0), axis=0, keepdims=True)
            for k, w in enumerate(ids):
                gath[q, pl.ds(w, 1), :] = line[:, k * segs : (k + 1) * segs]

    def gather_step(i, carry):
        gather_wells(4 * i, 4)
        return carry

    fours = (count + 1) // 4
    lax.fori_loop(0, fours, gather_step, 0)

    @pl.when(count > 4 * fours)
    def _():
        gather_wells(4 * fours, 2)

    vals = [gath[q, 0:wells, :] for q in range(len(fields))]
    props = mobility_of(vals[0], vals[3], vals[1], vals[4], vals[2], vals[5])
    drop = vals[0] - seg_p[...]
    ddrop = vals[3] - seg_d[...]
    weight = wi[...]
    total = jnp.zeros((wells, segs), F32)
    dtotal = jnp.zeros((wells, segs), F32)
    line = guides
    for a in range(3):
        mob, dmob = props[a][0], props[a][1]
        rate = jnp.where(owned, weight * mob * drop, 0.0)
        drate = jnp.where(owned, weight * (dmob * drop + mob * ddrop), 0.0)
        total = total + rate
        dtotal = dtotal + drate
        rates[a, 0:wells, :] = rate
        rates[3 + a, 0:wells, :] = drate
        of_well = jnp.sum(rate, axis=1, keepdims=True)
        line = jnp.where(spot == a * wells, of_well, line)
    line = jnp.sum(line, axis=0, keepdims=True)
    lines = jnp.concatenate([line, groups], axis=0)
    for y in range(gy):
        both = jnp.concatenate(
            [total[y * share : (y + 1) * share], dtotal[y * share : (y + 1) * share]], axis=0
        )
        send[pl.ds(xi * gy + y, 1), 0 : 2 * share, :] = both[None]
    for to in range(gx * gy):
        send[to, chunk - 2 : chunk, :] = lines


def cells_kernel(
    press,
    satur,
    pore,
    trans,
    direc,
    parent,
    seg_p,
    seg_d,
    head,
    inner,
    reach,
    known,
    edges,
    inside_pair,
    between_pairs,
    mobs,
    base,
):
    layers, cols, rows = press.shape
    chunks = cols // 8
    wells, segs = seg_p.shape
    share = reach.shape[0]
    start = lax.axis_index("gy") * share

    eye = iota((cols, rows), 0) == iota((cols, rows), 1)
    fields = [press, satur.at[0], satur.at[1], direc.at[0], direc.at[1], direc.at[2]]
    for side in range(4):
        lines = fields + [trans.at[side // 2]]
        for q, field in enumerate(lines):
            for z in range(layers):
                if q == 6 and side % 2 == 0:
                    line = jnp.zeros((1, rows), F32)
                elif side < 2:
                    line = field[z, 0:1, :] if side == 0 else field[z, cols - 1 : cols, :]
                else:
                    at = 0 if side == 2 else rows - 1
                    line = column_to_row(eye, field[z, :, at : at + 1])
                edges[side, q * layers + z : q * layers + z + 1, :] = line
    even = lax.rem(lax.axis_index("gy"), 2) == 0
    inside_pair[...] = jnp.where(even, edges[3], edges[2])
    between_pairs[...] = jnp.where(even, edges[2], edges[3])

    sub, lane = iota((segs, segs), 0), iota((segs, segs), 1)
    pad = jnp.zeros((10, segs), F32)
    mine = pl.ds(start, share)
    p_own, d_own = seg_p[mine, :], seg_d[mine, :]
    reaches, aboves, daboves = [], [], []
    for i in range(share):
        link = sub == parent[pl.ds(start + i, 1), :]
        reaches.append(jnp.where(link | (sub == lane), 1.0, 0.0).astype(BF16))
        lines = split(p_own[i : i + 1], 3) + split(d_own[i : i + 1], 3) + [pad]
        lines = jnp.concatenate(lines, axis=0).astype(BF16)
        found = dot(lines, jnp.where(link, 1.0, 0.0).astype(BF16))
        aboves.append(found[0:1] + found[1:2] + found[2:3])
        daboves.append(found[3:4] + found[4:5] + found[5:6])
    above, dabove = jnp.concatenate(aboves, axis=0), jnp.concatenate(daboves, axis=0)
    first = iota((share, segs), 1) == 0
    known[0:share, :] = jnp.where(first, p_own, p_own - above - head[mine, :])
    known[share : 2 * share, :] = jnp.where(first, d_own, d_own - dabove)

    for c in range(chunks):
        at = slice(8 * c, 8 * c + 8)
        for z in range(layers):
            p, dp = press[z, at, :], direc[0, z, at, :]
            props = mobility_of(
                p, dp, satur[0, z, at, :], direc[1, z, at, :], satur[1, z, at, :], direc[2, z, at, :]
            )
            rock = 1.0 + ROCK_COMP * (p - 1.0)
            drock = ROCK_COMP * dp
            pv = pore[z, at, :]
            for a in range(3):
                mob, dmob, mass, dmass = props[a]
                mobs[a, z, at, :] = mob
                mobs[3 + a, z, at, :] = dmob
                base[a, z, at, :] = pv * (rock * mass)
                base[3 + a, z, at, :] = pv * (drock * mass + rock * dmass)

    sub = iota((8, rows), 0)
    lane = iota((8, rows), 1)
    levels = (segs - 1).bit_length()
    refs = [press, direc.at[0]] + [mobs.at[k] for k in range(6)]

    def load(c):
        held = [[ref[z, 8 * c : 8 * c + 8, :] for ref in refs] for z in range(layers)]
        return held, [[pltpu.roll(x, 7, 0) for x in line] for line in held]

    before = [[jnp.zeros((8, rows), F32)] * layers for _ in range(6)]
    now, up = load(0)
    for c in range(chunks):
        at = slice(8 * c, 8 * c + 8)
        last_chunk = c == chunks - 1
        if not last_chunk:
            later, up_later = load(c + 1)
        sums = []
        for z in range(layers):
            if last_chunk:
                nexts = up[z]
            else:
                nexts = [jnp.where(sub == 7, x, y) for x, y in zip(up_later[z], up[z])]
            sides = [pltpu.roll(x, rows - 1, 1) for x in now[z]]
            p, dp = now[z][0:2]
            t_col, t_row = trans[0, z, at, :], trans[1, z, at, :]
            if last_chunk:
                t_col = jnp.where(sub == 7, 0.0, t_col)
            t_row = jnp.where(lane == rows - 1, 0.0, t_row)
            col = face_terms(t_col, p - nexts[0], dp - nexts[1])
            row = face_terms(t_row, p - sides[0], dp - sides[1])
            divergence = []
            for a in range(3):
                m, dm = now[z][2 + a], now[z][5 + a]
                flux_col = face_flux(col, m, dm, nexts[2 + a], nexts[5 + a])
                flux_row = face_flux(row, m, dm, sides[2 + a], sides[5 + a])
                both = []
                for t in (0, 1):
                    f, g = flux_col[t], flux_row[t]
                    rolled = pltpu.roll(f, 1, 0)
                    down = jnp.where(sub == 0, before[3 * t + a][z], rolled)
                    before[3 * t + a][z] = rolled
                    both.append(base[3 * t + a, z, at, :] + (f - down) + (g - pltpu.roll(g, 1, 1)))
                divergence.append(both)
            sums.append(divergence)
        for z in range(layers - 1):
            dpot = now[z][1] - now[z + 1][1]
            t_lay = trans[2, z, at, :]
            for a in range(3):
                pot = now[z][0] - now[z + 1][0] + DENSITY[a] * GRAVITY
                terms = face_terms(t_lay, pot, dpot)
                flux = face_flux(
                    terms, now[z][2 + a], now[z][5 + a], now[z + 1][2 + a], now[z + 1][5 + a]
                )
                for t in (0, 1):
                    sums[z][a][t] = sums[z][a][t] + flux[t]
                    sums[z + 1][a][t] = sums[z + 1][a][t] - flux[t]
        for z in range(layers):
            for a in range(3):
                for t in (0, 1):
                    inner[3 * t + a, z, at, :] = sums[z][a][t]
        if not last_chunk:
            now, up = later, up_later
        if c % 2 == 1 and c // 2 < levels:
            for i in range(share):
                reaches[i] = jnp.minimum(dot(reaches[i], reaches[i]), 1.0).astype(BF16)
    for level in range(chunks // 2, levels):
        for i in range(share):
            reaches[i] = jnp.minimum(dot(reaches[i], reaches[i]), 1.0).astype(BF16)
    for i in range(share):
        reach[i] = reaches[i]


def scatter_kernel(
    inner,
    old_mass,
    rates,
    rowloc,
    lxs,
    acc,
    packed,
    active,
):
    layers, cols, rows = acc.shape[1:]
    cells = layers * cols
    wells, segs = rates.shape[1] - 8, rates.shape[2]
    count = list_wells(rowloc[0:wells, :] >= 0, active)
    packed[...] = rates[0, wells + 4 : wells + 4 + packed.shape[0], :]

    for k in range(6):
        acc[k] = inner[k] - old_mass[k] if k < 3 else inner[k]

    sub_row = iota((rows, 4 * segs), 0)
    sub_lx = iota((cells, 4 * segs), 0)

    def scatter_wells(i, carry):
        ids = [active[1 + 4 * i + k] for k in range(4)]
        row = jnp.concatenate([rowloc[pl.ds(w, 1), :] for w in ids], axis=1)
        lx = jnp.concatenate([lxs[pl.ds(w, 1), :] for w in ids], axis=1)
        at = sub_row == row
        hot = jnp.where(sub_lx == lx, 1.0, 0.0).astype(BF16)
        hot = jnp.concatenate([hot, hot], axis=1)
        for q in range(0, 6, 2):
            both = []
            for k in (q, q + 1):
                rate = jnp.concatenate([rates[k, pl.ds(w, 1), :] for w in ids], axis=1)
                terms = [jnp.where(at, term, 0.0).astype(BF16) for term in split(rate, 2)]
                both.append(jnp.concatenate(terms, axis=1))
            part = dot(hot, jnp.concatenate(both, axis=0), NT)
            acc[q] = acc[q] + part[:, 0:rows].reshape(layers, cols, rows)
            acc[q + 1] = acc[q + 1] + part[:, rows : 2 * rows].reshape(layers, cols, rows)
        return carry

    lax.fori_loop(0, (count + 3) // 4, scatter_wells, 0)


def sides_kernel(
    acc, edges, inside_pair, between_pairs, out_hbm, dout_hbm, rims, out, turned, sems
):
    layers, cols, rows = out.shape[1:]
    gy, yi = lax.axis_size("gy"), lax.axis_index("gy")
    even = lax.rem(yi, 2) == 0
    one, other = inside_pair[...], between_pairs[...]
    prev, after = jnp.where(even, other, one), jnp.where(even, one, other)
    flux = outer_flux(edges[2], edges[3], prev, after, yi > 0, yi < gy - 1, layers)
    spare = jnp.zeros((128 - 12 * layers, rows), F32)
    turned[...] = jnp.concatenate(flux + [spare], axis=0).T
    lane = iota((cols, rows), 1)
    moves = []
    for k in range(6):
        for z in range(layers):
            j = 2 * layers * k + z
            before = turned[:, j : j + 1]
            behind = turned[:, j + layers : j + layers + 1]
            side = jnp.where(lane == 0, -before, jnp.where(lane == rows - 1, behind, 0.0))
            out[k, z] = acc[k, z] + side
            rims[k, 0, z] = out[k, z, 0:8, :]
            rims[k, 1, z] = out[k, z, cols - 8 : cols, :]
        final = out_hbm.at[k] if k < 3 else dout_hbm.at[k - 3]
        moves.append(pltpu.make_async_copy(out.at[k], final, sems.at[k]))
        moves[k].start()
    for move in moves:
        move.wait()


def finish_kernel(
    wells,
    out_before,
    dout_before,
    rims,
    reach,
    known,
    packed,
    edges,
    got,
    out_hbm,
    dout_hbm,
    seg_out_hbm,
    seg_dout_hbm,
    group_out_hbm,
    tiles,
    seg_out,
    seg_dout,
    group_out,
    sems,
):
    del out_before, dout_before
    layers = tiles.shape[3]
    cols = out_hbm.shape[2]
    share, segs = seg_out.shape
    gx, gy = lax.axis_size("gx"), lax.axis_size("gy")
    xi, yi = lax.axis_index("gx"), lax.axis_index("gy")
    chunk = got.shape[1]

    has_prev, has_next = xi > 0, xi < gx - 1
    prev, after = (
        got[pl.ds(jnp.where(inside, x * gy + yi, 0), 1), 0 : 7 * layers, :][0]
        for inside, x in ((has_prev, xi - 1), (has_next, xi + 1))
    )
    flux = outer_flux(edges[0], edges[1], prev, after, has_prev, has_next, layers)
    moves = []

    def write(src, dst):
        move = pltpu.make_async_copy(src, dst, sems.at[len(moves)])
        move.start()
        moves.append(move)

    for t, final in ((0, out_hbm), (1, dout_hbm)):
        for side, at in ((0, 0), (1, 7)):
            for a in range(3):
                k = 3 * t + a
                for z in range(layers):
                    tiles[t, side, a, z] = rims[k, side, z]
                    f = flux[k][side * layers + z : side * layers + z + 1]
                    line = rims[k, side, z, at : at + 1, :]
                    tiles[t, side, a, z, at : at + 1, :] = line - f if side == 0 else line + f
            write(tiles.at[t, side], final.at[:, :, pl.ds(side * (cols - 8), 8), :])

    total = got[xi * gy, 0 : 2 * share, :]
    for y in range(1, gy):
        total = total + got[xi * gy + y, 0 : 2 * share, :]

    lines, numbers = [], []
    for x in range(gx):
        line = got[x * gy, chunk - 2 : chunk - 1, :]
        more = line
        for y in range(1, gy):
            more = more + got[x * gy + y, chunk - 2 : chunk - 1, :]
        lines.append(jnp.where(iota((1, 128), 1) < 3 * wells, more, line))
        numbers.append(got[x * gy, chunk - 1 : chunk, :])
    columns = jnp.concatenate(lines + numbers + [jnp.zeros((128 - 2 * gx, 128), F32)], axis=0).T
    group_sums = [jnp.zeros((wells, 128), F32)] * 4
    for x in range(gx):
        member = columns[0:wells, gx + x : gx + x + 1] == iota((wells, 128), 1).astype(F32)
        for a in range(4):
            values = columns[a * wells : (a + 1) * wells, x : x + 1]
            group_sums[a] = group_sums[a] + jnp.where(member, values, 0.0)
    for a in range(3):
        group_out[a : a + 1, :] = jnp.sum(group_sums[a], axis=0, keepdims=True)
    write(group_out, group_out_hbm)
    guide_total = jnp.sum(group_sums[3], axis=0, keepdims=True)

    flows, dflows = [], []
    pad = jnp.zeros((10, segs), F32)
    for i in range(share):
        lines = split(total[i : i + 1], 3) + split(total[share + i : share + i + 1], 3) + [pad]
        flow = dot(jnp.concatenate(lines, axis=0).astype(BF16), reach[i], NT)
        flows.append(flow[0:1] + flow[1:2] + flow[2:3])
        dflows.append(flow[3:4] + flow[4:5] + flow[5:6])
    flow, dflow = jnp.concatenate(flows, axis=0), jnp.concatenate(dflows, axis=0)
    column = [packed[:, k : k + 1] for k in range(5)]
    member = column[2] == iota((share, 128), 1).astype(F32)
    of_group = jnp.sum(jnp.where(member, guide_total, 0.0), axis=1, keepdims=True)
    target = column[3] * column[1] / of_group
    by_rate = column[0] == 1.0
    first = iota((share, segs), 1) == 0
    limit, dlimit = known[0:share, :], known[share : 2 * share, :]
    root = jnp.where(by_rate, RATE_SCALE * (flow - target), limit - column[4])
    droot = jnp.where(by_rate, RATE_SCALE * dflow, dlimit)
    seg_out[...] = jnp.where(first, root, limit - FRICTION * flow)
    seg_dout[...] = jnp.where(first, droot, dlimit - FRICTION * dflow)
    write(seg_out, seg_out_hbm)
    write(seg_dout, seg_dout_hbm)
    for move in moves:
        move.wait()


VMEM = pl.BlockSpec(memory_space=pltpu.VMEM)
ANY = pl.BlockSpec(memory_space=pl.ANY)


def params(mebibytes):
    return pltpu.CompilerParams(vmem_limit_bytes=mebibytes * 1024 * 1024)


def per_device(
    pressure,
    saturations,
    old_mass,
    pore_volume,
    transmissibility,
    direction,
    seg_pressure,
    seg_direction,
    perf_cell,
    well_index,
    parent,
    seg_head,
    well_mode,
    bhp_limit,
    guide_rate,
    group_of,
    group_target,
):
    layers, cols, rows = pressure.shape
    wells, segs = seg_pressure.shape
    cells = layers * cols
    gx, gy = lax.axis_size("gx"), lax.axis_size("gy")
    share = wells // gy
    edge_rows = 7 * layers
    chunk = 2 + max(2 * share, edge_rows)
    shape = jax.ShapeDtypeStruct

    guide_line = guide_rate.reshape(1, wells)
    group_line = group_of.reshape(1, wells)
    send, rates, rowloc, lxs = pl.pallas_call(
        functools.partial(wells_kernel, rows * gy),
        out_shape=(
            shape((gx * gy, chunk, 128), F32),
            shape((6, wells + 8, segs), F32),
            shape((wells + 8, segs), jnp.int32),
            shape((wells + 8, segs), jnp.int32),
        ),
        in_specs=[ANY] * 13,
        out_specs=(VMEM,) * 4,
        scratch_shapes=[
            pltpu.VMEM((wells, segs), jnp.int32),
            pltpu.VMEM((layers, cols, rows), F32),
            pltpu.VMEM((2, layers, cols, rows), F32),
            pltpu.VMEM((3, layers, cols, rows), F32),
            pltpu.VMEM((wells, segs), F32),
            pltpu.VMEM((wells, segs), F32),
            pltpu.VMEM((wells, segs), F32),
            pltpu.VMEM((1, wells), F32),
            pltpu.VMEM((1, wells), jnp.int32),
            pltpu.VMEM((1, wells), jnp.int32),
            pltpu.VMEM((1, wells), F32),
            pltpu.VMEM((1, 128), F32),
            pltpu.VMEM((layers, 8, rows), F32),
            pltpu.VMEM((6, cells, 2 * rows), BF16),
            pltpu.VMEM((cells, rows), BF16),
            pltpu.VMEM((6, wells + 8, segs), F32),
            pltpu.SMEM((wells + 8,), jnp.int32),
            pltpu.SemaphoreType.DMA((13,)),
        ],
        compiler_params=params(56),
        name="wells",
    )(
        perf_cell,
        pressure,
        saturations,
        direction,
        seg_pressure,
        seg_direction,
        well_index,
        guide_line,
        group_line,
        well_mode.reshape(1, wells),
        bhp_limit.reshape(1, wells),
        group_target.reshape(1, 128),
        transmissibility,
    )

    got = lax.all_to_all(send, ("gx", "gy"), 0, 0, tiled=True)

    seg_head, rowloc = lax.optimization_barrier((seg_head, rowloc))

    inner, reach, known, edges, inside_pair, between_pairs = pl.pallas_call(
        cells_kernel,
        out_shape=(
            shape((6, layers, cols, rows), F32),
            shape((share, segs, segs), BF16),
            shape((2 * share, segs), F32),
            shape((4, edge_rows, 128), F32),
            shape((edge_rows, 128), F32),
            shape((edge_rows, 128), F32),
        ),
        in_specs=[VMEM] * 9,
        out_specs=(VMEM,) * 6,
        scratch_shapes=[
            pltpu.VMEM((6, layers, cols, rows), F32),
            pltpu.VMEM((6, layers, cols, rows), F32),
        ],
        compiler_params=params(32),
        cost_estimate=pl.CostEstimate(flops=300_000_000, bytes_accessed=4_000_000, transcendentals=400_000),
        name="cells",
    )(
        pressure,
        saturations,
        pore_volume,
        transmissibility,
        direction,
        parent,
        seg_pressure,
        seg_direction,
        seg_head,
    )

    def swap(x, first):
        pairs = [(i, i + 1) for i in range(first, gy - 1, 2)]
        return lax.ppermute(x, "gy", pairs + [(j, i) for i, j in pairs])

    inside_pair = swap(inside_pair, 0)
    between_pairs = swap(between_pairs, 1)

    cell_shape = shape((3, layers, cols, rows), F32)
    summed, packed = pl.pallas_call(
        scatter_kernel,
        out_shape=(shape((6, layers, cols, rows), F32), shape((share, 128), F32)),
        in_specs=[VMEM] * 5,
        out_specs=(VMEM, VMEM),
        scratch_shapes=[pltpu.SMEM((wells + 8,), jnp.int32)],
        compiler_params=params(32),
        cost_estimate=pl.CostEstimate(flops=300_000_000, bytes_accessed=4_000_000, transcendentals=0),
        name="scatter",
    )(
        inner,
        old_mass,
        rates,
        rowloc,
        lxs,
    )

    out, dout, rims = pl.pallas_call(
        sides_kernel,
        out_shape=(cell_shape, cell_shape, shape((6, 2, layers, 8, rows), F32)),
        in_specs=[VMEM] * 4,
        out_specs=(ANY, ANY, VMEM),
        scratch_shapes=[
            pltpu.VMEM((6, layers, cols, rows), F32),
            pltpu.VMEM((cols, 128), F32),
            pltpu.SemaphoreType.DMA((6,)),
        ],
        compiler_params=params(32),
        cost_estimate=pl.CostEstimate(flops=3_000_000, bytes_accessed=4_000_000, transcendentals=10_000),
        name="sides",
    )(summed, edges, inside_pair, between_pairs)

    out, dout, seg_out, seg_dout, groups = pl.pallas_call(
        functools.partial(finish_kernel, wells),
        out_shape=(
            cell_shape,
            cell_shape,
            shape((share, segs), F32),
            shape((share, segs), F32),
            shape((3, 128), F32),
        ),
        in_specs=[ANY] * 2 + [VMEM] * 6,
        out_specs=(ANY,) * 5,
        input_output_aliases={0: 0, 1: 1},
        scratch_shapes=[
            pltpu.VMEM((2, 2, 3, layers, 8, rows), F32),
            pltpu.VMEM((share, segs), F32),
            pltpu.VMEM((share, segs), F32),
            pltpu.VMEM((3, 128), F32),
            pltpu.SemaphoreType.DMA((7,)),
        ],
        compiler_params=params(32),
        name="finish",
    )(out, dout, rims, reach, known, packed, edges, got)
    return out, dout, seg_out, seg_dout, groups


def solution(mesh):
    placed = (
        P(None, "gx", "gy"),
        P(None, None, "gx", "gy"),
        P(None, None, "gx", "gy"),
        P(None, "gx", "gy"),
        P(None, None, "gx", "gy"),
        P(None, None, "gx", "gy"),
        P("gx", None),
        P("gx", None),
        P("gx", None),
        P("gx", None),
        P("gx", None),
        P("gx", None),
        P("gx"),
        P("gx"),
        P("gx"),
        P("gx", None),
        P(),
    )
    return jax.shard_map(
        per_device,
        mesh=mesh,
        in_specs=placed,
        out_specs=(
            P(None, None, "gx", "gy"),
            P(None, None, "gx", "gy"),
            P(("gx", "gy"), None),
            P(("gx", "gy"), None),
            P(),
        ),
        check_vma=False,
    )
```

time: 427 us -> 23 us (0.05)
  local copies, waits for them, and re-layouts: 233 us -> 0.07 us
  other arithmetic: 93.7 us -> 0 us
  blocking collectives: 75.7 us -> 0 us
  Pallas kernels: 0 us -> 9.5 us
  matrix products: 9.39 us -> 0 us
    gather x6 -> x0, local copies, waits for them, and re-layouts: 169 us -> none  [the longest x2 68.8 us: equations(): above = jnp.take_along_axis(seg_vals, parent, axis=1)]
    psum x3 -> x0, blocking collectives: 75.7 us -> none  [the longest x1 36.8 us: per_device(): group_rates = lax.psum(rates_part, ('gx', 'gy'))]
    scatter-add x2 -> x0, other arithmetic: 73.5 us -> none  [local_terms(): residual = residual.reshape(3, -1).at[:, flat_cell.reshape(-1)].add(rates...]
    unnamed x49 -> x26, local copies, waits for them, and re-layouts: 24.4 us -> 0.07 us
    slice x11 -> x0, local copies, waits for them, and re-layouts: 19.7 us -> none  [the longest x2 17.1 us: local_terms(): mobil_in = mobility[:, :, 1:-1, 1:-1]]
    sub x2 -> x0, local copies, waits for them, and re-layouts: 18.1 us -> none  [local_terms(): residual + jnp.pad(flux_layers, ((0, 0), (0, 1), (0, 0), (0, 0)))]
    ppermute x4 -> x2, starting transfers between devices: 11.3 us -> 0.97 us  [swap(): return lax.ppermute(x, 'gy', pairs + [(j, i) for i, j in pairs])]
    pallas_call x0 -> x5, Pallas kernels: none -> 9.5 us  [the longest x1 3.12 us: per_device(): pl.pallas_call(cells_kernel, out_shape=(shape((6, layers, cols, rows), F3...]
  transfers between devices with their start and end apart: 4 -> 3, of which waited for: 0 -> 1; matrix products, arithmetic and copies ran while one was open for 18% -> 0% of each run, Pallas kernels for 0% -> 23%
where the time goes in v1:
time: 23 us
  Pallas kernels  9.5 us (41%)
  starting transfers between devices  8.68 us (38%)
  waiting for transfers between devices  3.82 us (17%)
  between operations  0.9 us (4%)
    all_to_all x1, starting transfers between devices, per_device(): got = lax.all_to_all(send, ('gx', 'gy'), 0, 0, tiled=True)  7.71 us
    all_to_all x1, waiting for transfers between devices, per_device(): got = lax.all_to_all(send, ('gx', 'gy'), 0, 0, tiled=True)  3.81 us
    pallas_call x1, Pallas kernels, per_device(): pl.pallas_call(cells_kernel, out_shape=(shape((6, layers, cols, rows), F3...  3.12 us
    pallas_call x1, Pallas kernels, per_device(): pl.pallas_call(functools.partial(wells_kernel, rows * gy), out_shape=(sha...  3.04 us
    pallas_call x1, Pallas kernels, per_device(): pl.pallas_call(sides_kernel, out_shape=(cell_shape, cell_shape, shape((6,...  1.38 us
    pallas_call x1, Pallas kernels, per_device(): pl.pallas_call(functools.partial(finish_kernel, wells), out_shape=(cell_s...  1.08 us
    ppermute x2, starting transfers between devices, swap(): return lax.ppermute(x, 'gy', pairs + [(j, i) for i, j in pairs])  0.97 us
    pallas_call x1, Pallas kernels, per_device(): pl.pallas_call(scatter_kernel, out_shape=(shape((6, layers, cols, rows),...  0.89 us
  transfers between devices with their start and end apart: 3, of which 1 were waited for; matrix products, arithmetic and copies ran while one was open for 0% of the time, Pallas kernels for 23%

profile of v1, /device:TPU:0, one launch (start us, length us, event | category | flops | bytes accessed | tf_op | source)
XLA Modules:
  0.0 23.0 jit_solution(14552518440363715623)
XLA Ops:
  0.6 0.0 copy-start.1
  0.6 0.0 copy-start.2
  0.7 0.0 copy-start.5
  0.7 0.0 copy-start.7
  0.7 0.0 copy-start.8
  0.7 0.0 copy-start.11
  0.7 0.0 copy-start.12
  0.7 3.0 %wells.1 = (f32[32,16,128]{2,1,0:T(8,128)}, f32[6,40,128]{2,1,0:T(8,128)}, s32[40,128]{1,0:T(8,128)}, s32[40,128]{1,0:T(8,128)}) custom-call(s32[32,128]{1,0:T(8,128)} %perf_hbm.1, f32[2,128,128]{2,1,0:T(8,128)} %press.1, f32[2,2,128,128]{3,2,1,0:T(8,128)} %satur.1, f32[3,2,128,128]{3,2,1,0:T(8,128)} %direc.1, f32[32,128]{1,0:T(8,128)} %seg_p.1, ...), custom_call_target="tpu_custom_call" | custom-call | tf_op jit(solution)/shard_map/wells/pallas_call | solution.py:681
  3.8 0.0 copy-start
  3.8 0.0 copy-start.3
  3.8 7.7 %all-to-all-start = ((f32[32,16,128]{2,1,0:T(8,128)}), f32[32,16,128]{2,1,0:T(8,128)S(1)}, u32[]{:S(2)}, u32[]{:S(2)}) async-start(f32[32,16,128]{2,1,0:T(8,128)} %get-tuple-element.38), calls=%async_computation | async-start | bytes 524288 | tf_op jit(solution)/shard_map/all_to_all | solution.py:729
  11.5 0.0 copy-done.1
  11.5 0.0 copy-done.2
  11.5 0.0 copy-done.5
  11.5 0.0 copy-done.7
  11.5 0.0 copy-done.8
  11.5 0.0 copy-done.11
  11.6 0.0 copy-done.12
  11.6 0.0 copy-done
  11.6 0.0 copy-done.3
  11.6 0.0 copy-start.4
  11.6 0.0 copy-start.6
  11.6 0.0 copy-start.9
  11.6 0.0 copy-start.10
  11.6 3.1 %cells.1 = (f32[6,2,128,128]{3,2,1,0:T(8,128)S(1)}, bf16[4,128,128]{2,1,0:T(8,128)(2,1)S(1)}, f32[8,128]{1,0:T(8,128)S(1)}, f32[4,14,128]{2,1,0:T(8,128)S(1)}, f...) custom-call(f32[2,128,128]{2,1,0:T(8,128)S(1)} %copy-done.3, f32[2,2,128,128]{3,2,1,0:T(8,128)S(1)} %copy-done.2, ...), custom_call_target="tpu_custom_call" | custom-call | flops 300000000 | bytes 4000000 | tf_op jit(solution)/shard_map/cells/pallas_call | solution.py:733
  14.8 0.3 %collective-permute-start = (f32[14,128]{1,0:T(8,128)S(1)}, f32[14,128]{1,0:T(8,128)S(1)}, u32[]{:S(2)}, u32[]{:S(2)}) collective-permute-start(f32[14,128]{1,0:T(8,128)S(1)} %get-tuple-element.30), channel_id=1, source_target_pairs={{0,1},{2,3},{4,5},{6,7},{1,0},{3,2},{5,4},{7,6},{8,9},{10,11},{12,... | collective-permute-start | bytes 21512 | tf_op jit(solution)/shard_map/ppermute | solution.py:766
  15.1 0.6 %collective-permute-start.1 = (f32[14,128]{1,0:T(8,128)S(1)}, f32[14,128]{1,0:T(8,128)S(1)}, u32[]{:S(2)}, u32[]{:S(2)}) collective-permute-start(f32[14,128]{1,0:T(8,128)S(1)} %get-tuple-element.31), channel_id=1, source_target_pairs={{1,2},{3,4},{5,6},{2,1},{4,3},{6,5},{9,10},{11,12},{13,14},{10,9},... | collective-permute-start | bytes 21512 | tf_op jit(solution)/shard_map/ppermute | solution.py:766
  15.7 0.0 copy-done.4
  15.7 0.0 copy-done.6
  15.8 0.0 copy-done.9
  15.8 0.0 copy-done.10
  15.8 0.9 %scatter.1 = (f32[6,2,128,128]{3,2,1,0:T(8,128)S(1)}, f32[4,128]{1,0:T(4,128)S(1)}) custom-call(f32[6,2,128,128]{3,2,1,0:T(8,128)S(1)} %get-tuple-element.24.inner, f32[3,2,128,128]{3,2,1,0:T(8,128)S(1)} %copy-done.4, f32[6,40,128]{2,1,0:T(8,128)S(1)} %copy-done.6, s32[40,128]{1,0:T(8,128)S(1)} %copy-done.9, s32[40,128]{1,0:T(8,128)S(1)} %copy-done.10), custom_call_target="tpu_custom_call" | custom-call | flops 300000000 | bytes 4000000 | tf_op jit(solution)/shard_map/scatter/pallas_call | solution.py:772
  16.7 0.0 collective-permute-done.inside_pair
  16.7 0.0 collective-permute-done.1.between_pairs
  16.7 1.4 %sides.1 = (f32[3,2,128,128]{3,2,1,0:T(8,128)}, f32[3,2,128,128]{3,2,1,0:T(8,128)}, f32[6,2,2,8,128]{4,3,2,1,0:T(8,128)S(1)}) custom-call(f32[6,2,128,128]{3,2,1,0:T(8,128)S(1)} %get-tuple-element.28.acc, f32[4,14,128]{2,1,0:T(8,128)S(1)} %get-tuple-element.29.edges, f32[14,128]{1,0:T(8,128)S(1)} %collective-permute-done.inside_pair, ...), custom_call_target="tpu_custom_call" | custom-call | flops 3000000 | bytes 4000000 | tf_op jit(solution)/shard_map/sides/pallas_call | solution.py:789
  18.1 3.8 %all-to-all-done.got = f32[32,16,128]{2,1,0:T(8,128)S(1)} async-done(((f32[32,16,128]{2,1,0:T(8,128)}), f32[32,16,128]{2,1,0:T(8,128)S(1)}, u32[]{:S(2)}, u32[]{:S(2)}) %all-to-all-start) | async-done | bytes 262176 | tf_op jit(solution)/shard_map/all_to_all | solution.py:729
  21.9 1.1 %finish.1 = (f32[3,2,128,128]{3,2,1,0:T(8,128)}, f32[3,2,128,128]{3,2,1,0:T(8,128)}, f32[4,128]{1,0:T(4,128)}, f32[4,128]{1,0:T(4,128)}, f32[3,128]{1,0:T(4,128)}) custom-call(f32[3,2,128,128]{3,2,1,0:T(8,128)} %get-tuple-element.32.out_before, f32[3,2,128,128]{3,2,1,0:T(8,128)} %get-tuple-element.33.dout_before, ...), custom_call_target="tpu_custom_call", output_to_operand_aliasing={{0}: (0, {}), {1}: (1, {})} | custom-call | tf_op jit(solution)/shard_map/finish/pallas_call | solution.py:804
Async XLA Ops:
  0.6 10.9 %copy-start.1 = (f32[3,2,128,128]{3,2,1,0:T(8,128)S(1)}, f32[3,2,128,128]{3,2,1,0:T(8,128)}, u32[]{:S(2)}) copy-start(f32[3,2,128,128]{3,2,1,0:T(8,128)} %direc.1) | copy-start | bytes 1179652
  0.6 10.9 %copy-start.2 = (f32[2,2,128,128]{3,2,1,0:T(8,128)S(1)}, f32[2,2,128,128]{3,2,1,0:T(8,128)}, u32[]{:S(2)}) copy-start(f32[2,2,128,128]{3,2,1,0:T(8,128)} %satur.1) | copy-start | bytes 786436
  0.7 10.9 %copy-start.5 = (f32[2,128,128]{2,1,0:T(8,128)S(1)}, f32[2,128,128]{2,1,0:T(8,128)}, u32[]{:S(2)}) copy-start(f32[2,128,128]{2,1,0:T(8,128)} %pore.1) | copy-start | bytes 393220
  0.7 10.9 %copy-start.7 = (f32[32,128]{1,0:T(8,128)S(1)}, f32[32,128]{1,0:T(8,128)}, u32[]{:S(2)}) copy-start(f32[32,128]{1,0:T(8,128)} %seg_p.1) | copy-start | bytes 49156
  0.7 10.9 %copy-start.8 = (f32[32,128]{1,0:T(8,128)S(1)}, f32[32,128]{1,0:T(8,128)}, u32[]{:S(2)}) copy-start(f32[32,128]{1,0:T(8,128)} %seg_d.1) | copy-start | bytes 49156
  0.7 10.9 %copy-start.11 = (s32[32,128]{1,0:T(8,128)S(1)}, s32[32,128]{1,0:T(8,128)}, u32[]{:S(2)}) copy-start(s32[32,128]{1,0:T(8,128)} %parent.1) | copy-start | bytes 49156
  0.7 10.9 %copy-start.12 = (f32[32,128]{1,0:T(8,128)S(1)}, f32[32,128]{1,0:T(8,128)}, u32[]{:S(2)}) copy-start(f32[32,128]{1,0:T(8,128)} %head) | copy-start | bytes 49156
  3.8 7.8 %copy-start = (f32[3,2,128,128]{3,2,1,0:T(8,128)S(1)}, f32[3,2,128,128]{3,2,1,0:T(8,128)}, u32[]{:S(2)}) copy-start(f32[3,2,128,128]{3,2,1,0:T(8,128)} %trans.1) | copy-start | bytes 1179652
  3.8 7.8 %copy-start.3 = (f32[2,128,128]{2,1,0:T(8,128)S(1)}, f32[2,128,128]{2,1,0:T(8,128)}, u32[]{:S(2)}) copy-start(f32[2,128,128]{2,1,0:T(8,128)} %press.1) | copy-start | bytes 393220
  3.8 18.1 %all-to-all-start = ((f32[32,16,128]{2,1,0:T(8,128)}), f32[32,16,128]{2,1,0:T(8,128)S(1)}, u32[]{:S(2)}, u32[]{:S(2)}) async-start(f32[32,16,128]{2,1,0:T(8,128)} %get-tuple-element.38), calls=%async_computation | async-start | bytes 524288 | tf_op jit(solution)/shard_map/all_to_all | solution.py:729
  11.6 4.1 %copy-start.4 = (f32[3,2,128,128]{3,2,1,0:T(8,128)S(1)}, f32[3,2,128,128]{3,2,1,0:T(8,128)}, u32[]{:S(2)}) copy-start(f32[3,2,128,128]{3,2,1,0:T(8,128)} %old_mass.1) | copy-start | bytes 1179652
  11.6 4.1 %copy-start.6 = (f32[6,40,128]{2,1,0:T(8,128)S(1)}, f32[6,40,128]{2,1,0:T(8,128)}, u32[]{:S(2)}) copy-start(f32[6,40,128]{2,1,0:T(8,128)} %get-tuple-element.25.rates) | copy-start | bytes 368644
  11.6 4.1 %copy-start.9 = (s32[40,128]{1,0:T(8,128)S(1)}, s32[40,128]{1,0:T(8,128)}, u32[]{:S(2)}) copy-start(s32[40,128]{1,0:T(8,128)} %get-tuple-element.26.rowloc) | copy-start | bytes 61444
  11.6 4.1 %copy-start.10 = (s32[40,128]{1,0:T(8,128)S(1)}, s32[40,128]{1,0:T(8,128)}, u32[]{:S(2)}) copy-start(s32[40,128]{1,0:T(8,128)} %get-tuple-element.27.lxs) | copy-start | bytes 61444
  14.8 1.9 %collective-permute-start = (f32[14,128]{1,0:T(8,128)S(1)}, f32[14,128]{1,0:T(8,128)S(1)}, u32[]{:S(2)}, u32[]{:S(2)}) collective-permute-start(f32[14,128]{1,0:T(8,128)S(1)} %get-tuple-element.30), channel_id=1, source_target_pairs={{0,1},{2,3},{4,5},{6,7},{1,0},{3,2},{5,4},{7,6},{8,9},{10,11},{12,... | collective-permute-start | bytes 21512 | tf_op jit(solution)/shard_map/ppermute | solution.py:766
  15.1 1.6 %collective-permute-start.1 = (f32[14,128]{1,0:T(8,128)S(1)}, f32[14,128]{1,0:T(8,128)S(1)}, u32[]{:S(2)}, u32[]{:S(2)}) collective-permute-start(f32[14,128]{1,0:T(8,128)S(1)} %get-tuple-element.31), channel_id=1, source_target_pairs={{1,2},{3,4},{5,6},{2,1},{4,3},{6,5},{9,10},{11,12},{13,14},{10,9},... | collective-permute-start | bytes 21512 | tf_op jit(solution)/shard_map/ppermute | solution.py:766

commit v2 on v1

--- a/solution.py
+++ b/solution.py
@@ -194,7 +194,9 @@
     for move in moves:
         move.start()
 
-    moves[0].wait()
+    for move in moves:
+        move.wait()
+
     lx_all, row_all = located(perf[...], all_rows, yi * rows)
     owned = (row_all >= 0) & (row_all < rows)
     nowhere = jnp.full((8, segs), -1, jnp.int32)
@@ -204,8 +206,6 @@
     rowloc[wells : wells + 8, :] = nowhere
     count = list_wells(owned, active)
 
-    for move in moves[4:]:
-        move.wait()
     spot = iota((wells, 128), 1) - iota((wells, 128), 0)
     guides = jnp.where(spot == 3 * wells, as_column(guide[...]), 0.0)
     groups = jnp.where(spot == 0, as_column(group[...].astype(F32)), 0.0)
@@ -235,10 +235,7 @@
 
     edges = [[], []]
     fields = [press, satur.at[0], satur.at[1], direc.at[0], direc.at[1], direc.at[2]]
-    arrive = {0: 1, 1: 2, 3: 3}
     for q, field in enumerate(fields):
-        if q in arrive:
-            moves[arrive[q]].wait()
         block = field[...].reshape(cells, rows)
         terms = split(block, 3 if q == 0 else 2)
         held[q, :, 0:rows] = terms[0].astype(BF16)

time: 23 us -> 23.1 us (level)
  Pallas kernels: 9.5 us -> 9.76 us
    pallas_call x1, Pallas kernels: 3.04 us -> 3.3 us  [per_device(): pl.pallas_call(functools.partial(wells_kernel, rows * gy), out_shape=(sha...]
where the time goes in v2:
time: 23.1 us; the launch traced here: 23.2 us
  Pallas kernels  9.76 us (42%)
  starting transfers between devices  8.67 us (38%)
  waiting for transfers between devices  3.82 us (17%)
  between operations  0.9 us (4%)
    all_to_all x1, starting transfers between devices, per_device(): got = lax.all_to_all(send, ('gx', 'gy'), 0, 0, tiled=True)  7.71 us
    all_to_all x1, waiting for transfers between devices, per_device(): got = lax.all_to_all(send, ('gx', 'gy'), 0, 0, tiled=True)  3.81 us
    pallas_call x1, Pallas kernels, per_device(): pl.pallas_call(functools.partial(wells_kernel, rows * gy), out_shape=(sha...  3.3 us
    pallas_call x1, Pallas kernels, per_device(): pl.pallas_call(cells_kernel, out_shape=(shape((6, layers, cols, rows), F3...  3.12 us
    pallas_call x1, Pallas kernels, per_device(): pl.pallas_call(sides_kernel, out_shape=(cell_shape, cell_shape, shape((6,...  1.38 us
    pallas_call x1, Pallas kernels, per_device(): pl.pallas_call(functools.partial(finish_kernel, wells), out_shape=(cell_s...  1.08 us
    ppermute x2, starting transfers between devices, swap(): return lax.ppermute(x, 'gy', pairs + [(j, i) for i, j in pairs])  0.97 us
    pallas_call x1, Pallas kernels, per_device(): pl.pallas_call(scatter_kernel, out_shape=(shape((6, layers, cols, rows),...  0.89 us
  transfers between devices with their start and end apart: 3, of which 1 were waited for; matrix products, arithmetic and copies ran while one was open for 0% of the time, Pallas kernels for 23%

profile of v2, /device:TPU:0, one launch (start us, length us, event | category | flops | bytes accessed | tf_op | source)
XLA Modules:
  0.0 23.2 jit_solution(623956529409377183)
XLA Ops:
  0.6 0.0 copy-start.1
  0.6 0.0 copy-start.2
  0.7 0.0 copy-start.5
  0.7 0.0 copy-start.7
  0.7 0.0 copy-start.8
  0.7 0.0 copy-start.11
  0.7 0.0 copy-start.12
  0.7 3.3 %wells.1 = (f32[32,16,128]{2,1,0:T(8,128)}, f32[6,40,128]{2,1,0:T(8,128)}, s32[40,128]{1,0:T(8,128)}, s32[40,128]{1,0:T(8,128)}) custom-call(s32[32,128]{1,0:T(8,128)} %perf_hbm.1, f32[2,128,128]{2,1,0:T(8,128)} %press.1, f32[2,2,128,128]{3,2,1,0:T(8,128)} %satur.1, f32[3,2,128,128]{3,2,1,0:T(8,128)} %direc.1, f32[32,128]{1,0:T(8,128)} %seg_p.1, ...), custom_call_target="tpu_custom_call" | custom-call | tf_op jit(solution)/shard_map/wells/pallas_call | solution.py:678
  4.0 0.0 copy-start
  4.0 0.0 copy-start.3
  4.0 7.7 %all-to-all-start = ((f32[32,16,128]{2,1,0:T(8,128)}), f32[32,16,128]{2,1,0:T(8,128)S(1)}, u32[]{:S(2)}, u32[]{:S(2)}) async-start(f32[32,16,128]{2,1,0:T(8,128)} %get-tuple-element.38), calls=%async_computation | async-start | bytes 524288 | tf_op jit(solution)/shard_map/all_to_all | solution.py:726
  11.8 0.0 copy-done.1
  11.8 0.0 copy-done.2
  11.8 0.0 copy-done.5
  11.8 0.0 copy-done.7
  11.8 0.0 copy-done.8
  11.8 0.0 copy-done.11
  11.8 0.0 copy-done.12
  11.8 0.0 copy-done
  11.8 0.0 copy-done.3
  11.8 0.0 copy-start.4
  11.9 0.0 copy-start.6
  11.9 0.0 copy-start.9
  11.9 0.0 copy-start.10
  11.9 3.1 %cells.1 = (f32[6,2,128,128]{3,2,1,0:T(8,128)S(1)}, bf16[4,128,128]{2,1,0:T(8,128)(2,1)S(1)}, f32[8,128]{1,0:T(8,128)S(1)}, f32[4,14,128]{2,1,0:T(8,128)S(1)}, f...) custom-call(f32[2,128,128]{2,1,0:T(8,128)S(1)} %copy-done.3, f32[2,2,128,128]{3,2,1,0:T(8,128)S(1)} %copy-done.2, ...), custom_call_target="tpu_custom_call" | custom-call | flops 300000000 | bytes 4000000 | tf_op jit(solution)/shard_map/cells/pallas_call | solution.py:730
  15.0 0.3 %collective-permute-start = (f32[14,128]{1,0:T(8,128)S(1)}, f32[14,128]{1,0:T(8,128)S(1)}, u32[]{:S(2)}, u32[]{:S(2)}) collective-permute-start(f32[14,128]{1,0:T(8,128)S(1)} %get-tuple-element.30), channel_id=1, source_target_pairs={{0,1},{2,3},{4,5},{6,7},{1,0},{3,2},{5,4},{7,6},{8,9},{10,11},{12,... | collective-permute-start | bytes 21512 | tf_op jit(solution)/shard_map/ppermute | solution.py:763
  15.3 0.6 %collective-permute-start.1 = (f32[14,128]{1,0:T(8,128)S(1)}, f32[14,128]{1,0:T(8,128)S(1)}, u32[]{:S(2)}, u32[]{:S(2)}) collective-permute-start(f32[14,128]{1,0:T(8,128)S(1)} %get-tuple-element.31), channel_id=1, source_target_pairs={{1,2},{3,4},{5,6},{2,1},{4,3},{6,5},{9,10},{11,12},{13,14},{10,9},... | collective-permute-start | bytes 21512 | tf_op jit(solution)/shard_map/ppermute | solution.py:763
  16.0 0.0 copy-done.4
  16.0 0.0 copy-done.6
  16.0 0.0 copy-done.9
  16.0 0.0 copy-done.10
  16.0 0.9 %scatter.1 = (f32[6,2,128,128]{3,2,1,0:T(8,128)S(1)}, f32[4,128]{1,0:T(4,128)S(1)}) custom-call(f32[6,2,128,128]{3,2,1,0:T(8,128)S(1)} %get-tuple-element.24.inner, f32[3,2,128,128]{3,2,1,0:T(8,128)S(1)} %copy-done.4, f32[6,40,128]{2,1,0:T(8,128)S(1)} %copy-done.6, s32[40,128]{1,0:T(8,128)S(1)} %copy-done.9, s32[40,128]{1,0:T(8,128)S(1)} %copy-done.10), custom_call_target="tpu_custom_call" | custom-call | flops 300000000 | bytes 4000000 | tf_op jit(solution)/shard_map/scatter/pallas_call | solution.py:769
  16.9 0.0 collective-permute-done.inside_pair
  16.9 0.0 collective-permute-done.1.between_pairs
  16.9 1.4 %sides.1 = (f32[3,2,128,128]{3,2,1,0:T(8,128)}, f32[3,2,128,128]{3,2,1,0:T(8,128)}, f32[6,2,2,8,128]{4,3,2,1,0:T(8,128)S(1)}) custom-call(f32[6,2,128,128]{3,2,1,0:T(8,128)S(1)} %get-tuple-element.28.acc, f32[4,14,128]{2,1,0:T(8,128)S(1)} %get-tuple-element.29.edges, f32[14,128]{1,0:T(8,128)S(1)} %collective-permute-done.inside_pair, ...), custom_call_target="tpu_custom_call" | custom-call | flops 3000000 | bytes 4000000 | tf_op jit(solution)/shard_map/sides/pallas_call | solution.py:786
  18.3 3.8 %all-to-all-done.got = f32[32,16,128]{2,1,0:T(8,128)S(1)} async-done(((f32[32,16,128]{2,1,0:T(8,128)}), f32[32,16,128]{2,1,0:T(8,128)S(1)}, u32[]{:S(2)}, u32[]{:S(2)}) %all-to-all-start) | async-done | bytes 262176 | tf_op jit(solution)/shard_map/all_to_all | solution.py:726
  22.1 1.1 %finish.1 = (f32[3,2,128,128]{3,2,1,0:T(8,128)}, f32[3,2,128,128]{3,2,1,0:T(8,128)}, f32[4,128]{1,0:T(4,128)}, f32[4,128]{1,0:T(4,128)}, f32[3,128]{1,0:T(4,128)}) custom-call(f32[3,2,128,128]{3,2,1,0:T(8,128)} %get-tuple-element.32.out_before, f32[3,2,128,128]{3,2,1,0:T(8,128)} %get-tuple-element.33.dout_before, ...), custom_call_target="tpu_custom_call", output_to_operand_aliasing={{0}: (0, {}), {1}: (1, {})} | custom-call | tf_op jit(solution)/shard_map/finish/pallas_call | solution.py:801
Async XLA Ops:
  0.6 11.1 %copy-start.1 = (f32[3,2,128,128]{3,2,1,0:T(8,128)S(1)}, f32[3,2,128,128]{3,2,1,0:T(8,128)}, u32[]{:S(2)}) copy-start(f32[3,2,128,128]{3,2,1,0:T(8,128)} %direc.1) | copy-start | bytes 1179652
  0.6 11.1 %copy-start.2 = (f32[2,2,128,128]{3,2,1,0:T(8,128)S(1)}, f32[2,2,128,128]{3,2,1,0:T(8,128)}, u32[]{:S(2)}) copy-start(f32[2,2,128,128]{3,2,1,0:T(8,128)} %satur.1) | copy-start | bytes 786436
  0.7 11.1 %copy-start.5 = (f32[2,128,128]{2,1,0:T(8,128)S(1)}, f32[2,128,128]{2,1,0:T(8,128)}, u32[]{:S(2)}) copy-start(f32[2,128,128]{2,1,0:T(8,128)} %pore.1) | copy-start | bytes 393220
  0.7 11.1 %copy-start.7 = (f32[32,128]{1,0:T(8,128)S(1)}, f32[32,128]{1,0:T(8,128)}, u32[]{:S(2)}) copy-start(f32[32,128]{1,0:T(8,128)} %seg_p.1) | copy-start | bytes 49156
  0.7 11.1 %copy-start.8 = (f32[32,128]{1,0:T(8,128)S(1)}, f32[32,128]{1,0:T(8,128)}, u32[]{:S(2)}) copy-start(f32[32,128]{1,0:T(8,128)} %seg_d.1) | copy-start | bytes 49156
  0.7 11.1 %copy-start.11 = (s32[32,128]{1,0:T(8,128)S(1)}, s32[32,128]{1,0:T(8,128)}, u32[]{:S(2)}) copy-start(s32[32,128]{1,0:T(8,128)} %parent.1) | copy-start | bytes 49156
  0.7 11.1 %copy-start.12 = (f32[32,128]{1,0:T(8,128)S(1)}, f32[32,128]{1,0:T(8,128)}, u32[]{:S(2)}) copy-start(f32[32,128]{1,0:T(8,128)} %head) | copy-start | bytes 49156
  4.0 7.8 %copy-start = (f32[3,2,128,128]{3,2,1,0:T(8,128)S(1)}, f32[3,2,128,128]{3,2,1,0:T(8,128)}, u32[]{:S(2)}) copy-start(f32[3,2,128,128]{3,2,1,0:T(8,128)} %trans.1) | copy-start | bytes 1179652
  4.0 7.8 %copy-start.3 = (f32[2,128,128]{2,1,0:T(8,128)S(1)}, f32[2,128,128]{2,1,0:T(8,128)}, u32[]{:S(2)}) copy-start(f32[2,128,128]{2,1,0:T(8,128)} %press.1) | copy-start | bytes 393220
  4.0 18.1 %all-to-all-start = ((f32[32,16,128]{2,1,0:T(8,128)}), f32[32,16,128]{2,1,0:T(8,128)S(1)}, u32[]{:S(2)}, u32[]{:S(2)}) async-start(f32[32,16,128]{2,1,0:T(8,128)} %get-tuple-element.38), calls=%async_computation | async-start | bytes 524288 | tf_op jit(solution)/shard_map/all_to_all | solution.py:726
  11.8 4.1 %copy-start.4 = (f32[3,2,128,128]{3,2,1,0:T(8,128)S(1)}, f32[3,2,128,128]{3,2,1,0:T(8,128)}, u32[]{:S(2)}) copy-start(f32[3,2,128,128]{3,2,1,0:T(8,128)} %old_mass.1) | copy-start | bytes 1179652
  11.9 4.1 %copy-start.6 = (f32[6,40,128]{2,1,0:T(8,128)S(1)}, f32[6,40,128]{2,1,0:T(8,128)}, u32[]{:S(2)}) copy-start(f32[6,40,128]{2,1,0:T(8,128)} %get-tuple-element.25.rates) | copy-start | bytes 368644
  11.9 4.1 %copy-start.9 = (s32[40,128]{1,0:T(8,128)S(1)}, s32[40,128]{1,0:T(8,128)}, u32[]{:S(2)}) copy-start(s32[40,128]{1,0:T(8,128)} %get-tuple-element.26.rowloc) | copy-start | bytes 61444
  11.9 4.1 %copy-start.10 = (s32[40,128]{1,0:T(8,128)S(1)}, s32[40,128]{1,0:T(8,128)}, u32[]{:S(2)}) copy-start(s32[40,128]{1,0:T(8,128)} %get-tuple-element.27.lxs) | copy-start | bytes 61444
  15.0 1.9 %collective-permute-start = (f32[14,128]{1,0:T(8,128)S(1)}, f32[14,128]{1,0:T(8,128)S(1)}, u32[]{:S(2)}, u32[]{:S(2)}) collective-permute-start(f32[14,128]{1,0:T(8,128)S(1)} %get-tuple-element.30), channel_id=1, source_target_pairs={{0,1},{2,3},{4,5},{6,7},{1,0},{3,2},{5,4},{7,6},{8,9},{10,11},{12,... | collective-permute-start | bytes 21512 | tf_op jit(solution)/shard_map/ppermute | solution.py:763
  15.3 1.6 %collective-permute-start.1 = (f32[14,128]{1,0:T(8,128)S(1)}, f32[14,128]{1,0:T(8,128)S(1)}, u32[]{:S(2)}, u32[]{:S(2)}) collective-permute-start(f32[14,128]{1,0:T(8,128)S(1)} %get-tuple-element.31), channel_id=1, source_target_pairs={{1,2},{3,4},{5,6},{2,1},{4,3},{6,5},{9,10},{11,12},{13,14},{10,9},... | collective-permute-start | bytes 21512 | tf_op jit(solution)/shard_map/ppermute | solution.py:763

commit v3 on v1

--- a/solution.py
+++ b/solution.py
@@ -258,7 +258,7 @@
         edge = jnp.concatenate(edges[side], axis=0)
 
         @pl.when((there >= 0) & (there < gx))
-        def _(edge=edge, to=there * gy + yi):
+        def _(edge=edge, to=yi * gx + there):
             send[pl.ds(to, 1), 0 : 7 * layers, :] = edge[None]
 
     def gather_wells(at, width):
@@ -311,7 +311,7 @@
         both = jnp.concatenate(
             [total[y * share : (y + 1) * share], dtotal[y * share : (y + 1) * share]], axis=0
         )
-        send[pl.ds(xi * gy + y, 1), 0 : 2 * share, :] = both[None]
+        send[pl.ds(y * gx + xi, 1), 0 : 2 * share, :] = both[None]
     for to in range(gx * gy):
         send[to, chunk - 2 : chunk, :] = lines
 
@@ -569,7 +569,7 @@
 
     has_prev, has_next = xi > 0, xi < gx - 1
     prev, after = (
-        got[pl.ds(jnp.where(inside, x * gy + yi, 0), 1), 0 : 7 * layers, :][0]
+        got[pl.ds(jnp.where(inside, yi * gx + x, 0), 1), 0 : 7 * layers, :][0]
         for inside, x in ((has_prev, xi - 1), (has_next, xi + 1))
     )
     flux = outer_flux(edges[0], edges[1], prev, after, has_prev, has_next, layers)
@@ -591,18 +591,18 @@
                     tiles[t, side, a, z, at : at + 1, :] = line - f if side == 0 else line + f
             write(tiles.at[t, side], final.at[:, :, pl.ds(side * (cols - 8), 8), :])
 
-    total = got[xi * gy, 0 : 2 * share, :]
+    total = got[xi, 0 : 2 * share, :]
     for y in range(1, gy):
-        total = total + got[xi * gy + y, 0 : 2 * share, :]
+        total = total + got[y * gx + xi, 0 : 2 * share, :]
 
     lines, numbers = [], []
     for x in range(gx):
-        line = got[x * gy, chunk - 2 : chunk - 1, :]
+        line = got[x, chunk - 2 : chunk - 1, :]
         more = line
         for y in range(1, gy):
-            more = more + got[x * gy + y, chunk - 2 : chunk - 1, :]
+            more = more + got[y * gx + x, chunk - 2 : chunk - 1, :]
         lines.append(jnp.where(iota((1, 128), 1) < 3 * wells, more, line))
-        numbers.append(got[x * gy, chunk - 1 : chunk, :])
+        numbers.append(got[x, chunk - 1 : chunk, :])
     columns = jnp.concatenate(lines + numbers + [jnp.zeros((128 - 2 * gx, 128), F32)], axis=0).T
     group_sums = [jnp.zeros((wells, 128), F32)] * 4
     for x in range(gx):
@@ -726,7 +726,7 @@
         transmissibility,
     )
 
-    got = lax.all_to_all(send, ("gx", "gy"), 0, 0, tiled=True)
+    got = lax.all_to_all(send, ("gy", "gx"), 0, 0, tiled=True)
 
     seg_head, rowloc = lax.optimization_barrier((seg_head, rowloc))
 

time: 23 us -> 23.8 us (1.035)
  waiting for transfers between devices: 3.82 us -> 4.38 us
    all_to_all x1, waiting for transfers between devices: 3.81 us -> 4.38 us  [per_device(): got = lax.all_to_all(send, ('gy', 'gx'), 0, 0, tiled=True)]
where the time goes in v3:
time: 23.8 us; the launch traced here: 23.5 us
  Pallas kernels  9.5 us (40%)
  starting transfers between devices  8.68 us (36%)
  waiting for transfers between devices  4.38 us (18%)
  between operations  0.9 us (4%)
    all_to_all x1, starting transfers between devices, per_device(): got = lax.all_to_all(send, ('gy', 'gx'), 0, 0, tiled=True)  7.71 us
    all_to_all x1, waiting for transfers between devices, per_device(): got = lax.all_to_all(send, ('gy', 'gx'), 0, 0, tiled=True)  4.38 us
    pallas_call x1, Pallas kernels, per_device(): pl.pallas_call(cells_kernel, out_shape=(shape((6, layers, cols, rows), F3...  3.12 us
    pallas_call x1, Pallas kernels, per_device(): pl.pallas_call(functools.partial(wells_kernel, rows * gy), out_shape=(sha...  3.04 us
    pallas_call x1, Pallas kernels, per_device(): pl.pallas_call(sides_kernel, out_shape=(cell_shape, cell_shape, shape((6,...  1.38 us
    pallas_call x1, Pallas kernels, per_device(): pl.pallas_call(functools.partial(finish_kernel, wells), out_shape=(cell_s...  1.08 us
    ppermute x2, starting transfers between devices, swap(): return lax.ppermute(x, 'gy', pairs + [(j, i) for i, j in pairs])  0.97 us
    pallas_call x1, Pallas kernels, per_device(): pl.pallas_call(scatter_kernel, out_shape=(shape((6, layers, cols, rows),...  0.88 us
  transfers between devices with their start and end apart: 3, of which 1 were waited for; matrix products, arithmetic and copies ran while one was open for 0% of the time, Pallas kernels for 23%

profile of v3, /device:TPU:0, one launch (start us, length us, event | category | flops | bytes accessed | tf_op | source)
XLA Modules:
  0.0 23.5 jit_solution(6024654142387317344)
XLA Ops:
  0.6 0.0 copy-start.1
  0.6 0.0 copy-start.2
  0.7 0.0 copy-start.5
  0.7 0.0 copy-start.7
  0.7 0.0 copy-start.8
  0.7 0.0 copy-start.11
  0.7 0.0 copy-start.12
  0.7 3.0 %wells.1 = (f32[32,16,128]{2,1,0:T(8,128)}, f32[6,40,128]{2,1,0:T(8,128)}, s32[40,128]{1,0:T(8,128)}, s32[40,128]{1,0:T(8,128)}) custom-call(s32[32,128]{1,0:T(8,128)} %perf_hbm.1, f32[2,128,128]{2,1,0:T(8,128)} %press.1, f32[2,2,128,128]{3,2,1,0:T(8,128)} %satur.1, f32[3,2,128,128]{3,2,1,0:T(8,128)} %direc.1, f32[32,128]{1,0:T(8,128)} %seg_p.1, ...), custom_call_target="tpu_custom_call" | custom-call | tf_op jit(solution)/shard_map/wells/pallas_call | solution.py:681
  3.8 0.0 copy-start
  3.8 0.0 copy-start.3
  3.8 7.7 %all-to-all-start = ((f32[32,16,128]{2,1,0:T(8,128)}), f32[32,16,128]{2,1,0:T(8,128)S(1)}, u32[]{:S(2)}, u32[]{:S(2)}) async-start(f32[32,16,128]{2,1,0:T(8,128)} %get-tuple-element.38), calls=%async_computation | async-start | bytes 524288 | tf_op jit(solution)/shard_map/all_to_all | solution.py:729
  11.5 0.0 copy-done.1
  11.5 0.0 copy-done.2
  11.5 0.0 copy-done.5
  11.5 0.0 copy-done.7
  11.5 0.0 copy-done.8
  11.5 0.0 copy-done.11
  11.6 0.0 copy-done.12
  11.6 0.0 copy-done
  11.6 0.0 copy-done.3
  11.6 0.0 copy-start.4
  11.6 0.0 copy-start.6
  11.6 0.0 copy-start.9
  11.6 0.0 copy-start.10
  11.6 3.1 %cells.1 = (f32[6,2,128,128]{3,2,1,0:T(8,128)S(1)}, bf16[4,128,128]{2,1,0:T(8,128)(2,1)S(1)}, f32[8,128]{1,0:T(8,128)S(1)}, f32[4,14,128]{2,1,0:T(8,128)S(1)}, f...) custom-call(f32[2,128,128]{2,1,0:T(8,128)S(1)} %copy-done.3, f32[2,2,128,128]{3,2,1,0:T(8,128)S(1)} %copy-done.2, ...), custom_call_target="tpu_custom_call" | custom-call | flops 300000000 | bytes 4000000 | tf_op jit(solution)/shard_map/cells/pallas_call | solution.py:733
  14.8 0.3 %collective-permute-start = (f32[14,128]{1,0:T(8,128)S(1)}, f32[14,128]{1,0:T(8,128)S(1)}, u32[]{:S(2)}, u32[]{:S(2)}) collective-permute-start(f32[14,128]{1,0:T(8,128)S(1)} %get-tuple-element.30), channel_id=1, source_target_pairs={{0,1},{2,3},{4,5},{6,7},{1,0},{3,2},{5,4},{7,6},{8,9},{10,11},{12,... | collective-permute-start | bytes 21512 | tf_op jit(solution)/shard_map/ppermute | solution.py:766
  15.1 0.6 %collective-permute-start.1 = (f32[14,128]{1,0:T(8,128)S(1)}, f32[14,128]{1,0:T(8,128)S(1)}, u32[]{:S(2)}, u32[]{:S(2)}) collective-permute-start(f32[14,128]{1,0:T(8,128)S(1)} %get-tuple-element.31), channel_id=1, source_target_pairs={{1,2},{3,4},{5,6},{2,1},{4,3},{6,5},{9,10},{11,12},{13,14},{10,9},... | collective-permute-start | bytes 21512 | tf_op jit(solution)/shard_map/ppermute | solution.py:766
  15.7 0.0 copy-done.4
  15.7 0.0 copy-done.6
  15.8 0.0 copy-done.9
  15.8 0.0 copy-done.10
  15.8 0.9 %scatter.1 = (f32[6,2,128,128]{3,2,1,0:T(8,128)S(1)}, f32[4,128]{1,0:T(4,128)S(1)}) custom-call(f32[6,2,128,128]{3,2,1,0:T(8,128)S(1)} %get-tuple-element.24.inner, f32[3,2,128,128]{3,2,1,0:T(8,128)S(1)} %copy-done.4, f32[6,40,128]{2,1,0:T(8,128)S(1)} %copy-done.6, s32[40,128]{1,0:T(8,128)S(1)} %copy-done.9, s32[40,128]{1,0:T(8,128)S(1)} %copy-done.10), custom_call_target="tpu_custom_call" | custom-call | flops 300000000 | bytes 4000000 | tf_op jit(solution)/shard_map/scatter/pallas_call | solution.py:772
  16.7 0.0 collective-permute-done.inside_pair
  16.7 0.0 collective-permute-done.1.between_pairs
  16.7 1.4 %sides.1 = (f32[3,2,128,128]{3,2,1,0:T(8,128)}, f32[3,2,128,128]{3,2,1,0:T(8,128)}, f32[6,2,2,8,128]{4,3,2,1,0:T(8,128)S(1)}) custom-call(f32[6,2,128,128]{3,2,1,0:T(8,128)S(1)} %get-tuple-element.28.acc, f32[4,14,128]{2,1,0:T(8,128)S(1)} %get-tuple-element.29.edges, f32[14,128]{1,0:T(8,128)S(1)} %collective-permute-done.inside_pair, ...), custom_call_target="tpu_custom_call" | custom-call | flops 3000000 | bytes 4000000 | tf_op jit(solution)/shard_map/sides/pallas_call | solution.py:789
  18.1 4.4 %all-to-all-done.got = f32[32,16,128]{2,1,0:T(8,128)S(1)} async-done(((f32[32,16,128]{2,1,0:T(8,128)}), f32[32,16,128]{2,1,0:T(8,128)S(1)}, u32[]{:S(2)}, u32[]{:S(2)}) %all-to-all-start) | async-done | bytes 262176 | tf_op jit(solution)/shard_map/all_to_all | solution.py:729
  22.4 1.1 %finish.1 = (f32[3,2,128,128]{3,2,1,0:T(8,128)}, f32[3,2,128,128]{3,2,1,0:T(8,128)}, f32[4,128]{1,0:T(4,128)}, f32[4,128]{1,0:T(4,128)}, f32[3,128]{1,0:T(4,128)}) custom-call(f32[3,2,128,128]{3,2,1,0:T(8,128)} %get-tuple-element.32.out_before, f32[3,2,128,128]{3,2,1,0:T(8,128)} %get-tuple-element.33.dout_before, ...), custom_call_target="tpu_custom_call", output_to_operand_aliasing={{0}: (0, {}), {1}: (1, {})} | custom-call | tf_op jit(solution)/shard_map/finish/pallas_call | solution.py:804
Async XLA Ops:
  0.6 10.9 %copy-start.1 = (f32[3,2,128,128]{3,2,1,0:T(8,128)S(1)}, f32[3,2,128,128]{3,2,1,0:T(8,128)}, u32[]{:S(2)}) copy-start(f32[3,2,128,128]{3,2,1,0:T(8,128)} %direc.1) | copy-start | bytes 1179652
  0.6 10.9 %copy-start.2 = (f32[2,2,128,128]{3,2,1,0:T(8,128)S(1)}, f32[2,2,128,128]{3,2,1,0:T(8,128)}, u32[]{:S(2)}) copy-start(f32[2,2,128,128]{3,2,1,0:T(8,128)} %satur.1) | copy-start | bytes 786436
  0.7 10.9 %copy-start.5 = (f32[2,128,128]{2,1,0:T(8,128)S(1)}, f32[2,128,128]{2,1,0:T(8,128)}, u32[]{:S(2)}) copy-start(f32[2,128,128]{2,1,0:T(8,128)} %pore.1) | copy-start | bytes 393220
  0.7 10.9 %copy-start.7 = (f32[32,128]{1,0:T(8,128)S(1)}, f32[32,128]{1,0:T(8,128)}, u32[]{:S(2)}) copy-start(f32[32,128]{1,0:T(8,128)} %seg_p.1) | copy-start | bytes 49156
  0.7 10.9 %copy-start.8 = (f32[32,128]{1,0:T(8,128)S(1)}, f32[32,128]{1,0:T(8,128)}, u32[]{:S(2)}) copy-start(f32[32,128]{1,0:T(8,128)} %seg_d.1) | copy-start | bytes 49156
  0.7 10.9 %copy-start.11 = (s32[32,128]{1,0:T(8,128)S(1)}, s32[32,128]{1,0:T(8,128)}, u32[]{:S(2)}) copy-start(s32[32,128]{1,0:T(8,128)} %parent.1) | copy-start | bytes 49156
  0.7 10.9 %copy-start.12 = (f32[32,128]{1,0:T(8,128)S(1)}, f32[32,128]{1,0:T(8,128)}, u32[]{:S(2)}) copy-start(f32[32,128]{1,0:T(8,128)} %head) | copy-start | bytes 49156
  3.8 7.8 %copy-start = (f32[3,2,128,128]{3,2,1,0:T(8,128)S(1)}, f32[3,2,128,128]{3,2,1,0:T(8,128)}, u32[]{:S(2)}) copy-start(f32[3,2,128,128]{3,2,1,0:T(8,128)} %trans.1) | copy-start | bytes 1179652
  3.8 7.8 %copy-start.3 = (f32[2,128,128]{2,1,0:T(8,128)S(1)}, f32[2,128,128]{2,1,0:T(8,128)}, u32[]{:S(2)}) copy-start(f32[2,128,128]{2,1,0:T(8,128)} %press.1) | copy-start | bytes 393220
  3.8 18.7 %all-to-all-start = ((f32[32,16,128]{2,1,0:T(8,128)}), f32[32,16,128]{2,1,0:T(8,128)S(1)}, u32[]{:S(2)}, u32[]{:S(2)}) async-start(f32[32,16,128]{2,1,0:T(8,128)} %get-tuple-element.38), calls=%async_computation | async-start | bytes 524288 | tf_op jit(solution)/shard_map/all_to_all | solution.py:729
  11.6 4.1 %copy-start.4 = (f32[3,2,128,128]{3,2,1,0:T(8,128)S(1)}, f32[3,2,128,128]{3,2,1,0:T(8,128)}, u32[]{:S(2)}) copy-start(f32[3,2,128,128]{3,2,1,0:T(8,128)} %old_mass.1) | copy-start | bytes 1179652
  11.6 4.1 %copy-start.6 = (f32[6,40,128]{2,1,0:T(8,128)S(1)}, f32[6,40,128]{2,1,0:T(8,128)}, u32[]{:S(2)}) copy-start(f32[6,40,128]{2,1,0:T(8,128)} %get-tuple-element.25.rates) | copy-start | bytes 368644
  11.6 4.1 %copy-start.9 = (s32[40,128]{1,0:T(8,128)S(1)}, s32[40,128]{1,0:T(8,128)}, u32[]{:S(2)}) copy-start(s32[40,128]{1,0:T(8,128)} %get-tuple-element.26.rowloc) | copy-start | bytes 61444
  11.6 4.1 %copy-start.10 = (s32[40,128]{1,0:T(8,128)S(1)}, s32[40,128]{1,0:T(8,128)}, u32[]{:S(2)}) copy-start(s32[40,128]{1,0:T(8,128)} %get-tuple-element.27.lxs) | copy-start | bytes 61444
  14.8 1.9 %collective-permute-start = (f32[14,128]{1,0:T(8,128)S(1)}, f32[14,128]{1,0:T(8,128)S(1)}, u32[]{:S(2)}, u32[]{:S(2)}) collective-permute-start(f32[14,128]{1,0:T(8,128)S(1)} %get-tuple-element.30), channel_id=1, source_target_pairs={{0,1},{2,3},{4,5},{6,7},{1,0},{3,2},{5,4},{7,6},{8,9},{10,11},{12,... | collective-permute-start | bytes 21512 | tf_op jit(solution)/shard_map/ppermute | solution.py:766
  15.1 1.6 %collective-permute-start.1 = (f32[14,128]{1,0:T(8,128)S(1)}, f32[14,128]{1,0:T(8,128)S(1)}, u32[]{:S(2)}, u32[]{:S(2)}) collective-permute-start(f32[14,128]{1,0:T(8,128)S(1)} %get-tuple-element.31), channel_id=1, source_target_pairs={{1,2},{3,4},{5,6},{2,1},{4,3},{6,5},{9,10},{11,12},{13,14},{10,9},... | collective-permute-start | bytes 21512 | tf_op jit(solution)/shard_map/ppermute | solution.py:766
